TPU v7x, 32 devices: a whole 2x2x4 slice. The times are simulated.
32 devices in a mesh: dp: 16 (over z, y, x), tensor: 2 (over core).
Axes of the slice: x: 2, y: 2, z: 4, core: 2. Of those that a mesh axis runs over, the one named last changes fastest.
Arguments:
- normed: bfloat16 [1024, 1280], P('dp'), may hold values from -6 to 6
- residual_in: bfloat16 [1024, 1280], P('dp'), may hold values from -6 to 6
- w_up: bfloat16 [1280, 5120], P('dp', 'tensor'), may hold values from -0.15625 to 0.15625
- w_down: bfloat16 [5120, 1280], P('tensor', 'dp'), may hold values from -0.15625 to 0.15625
- final_gain: float32 [1280], replicated, may hold values from 0.1 to 1.9
- head_cols: bfloat16 [1280, 16], replicated, may hold values from -4 to 4
- sub_inputs: int32 [2048], P('tensor'), may hold values from 0 to 1279
- sub_hidden: int32 [2048], P('tensor'), may hold values from 0 to 5119, as said below
- panels: bfloat16 [2, 256, 2048], P(None, 'dp', 'tensor'), may hold values from -0.1001 to 0.1001, as said below
- inverses: bfloat16 [2, 256, 256], replicated, may hold values from -0.1001 to 2, as said below
Outputs:
- whitened: bfloat16 [1024, 16, 2048], P('dp', None, 'tensor')
Inputs may be any that keep to these rules, and one draw needn't show every extreme that they name: `sub_hidden`: window rows t * 1024 to (t + 1) * 1024 - 1 name hidden units t * 2560 to (t + 1) * 2560 - 1. `panels`: entry [q, c, r] is zero for r < (q + 1) * 256. `inverses`: each block is lower triangular with a positive diagonal.
All inputs are finite; a program needn't handle non-finite values.
Results may differ from a plain program's by a relative error of at most 0.0069.
Values may be sent and summed in bfloat16 or wider, within the bound.
A program may use at most 64 MiB of HBM per device.

v0:
```python
import jax
import jax.numpy as jnp
from jax import lax
from jax.sharding import PartitionSpec as P


def from_root(shard, axis, root):
    mine = lax.axis_index(axis) == root
    return lax.psum(jnp.where(mine, shard, jnp.zeros_like(shard)), axis)


def gelu_parts(values):
    normal_cdf = 0.5 * (1.0 + jax.scipy.special.erf(values * 0.7071067811865476))
    slope = normal_cdf + values * jnp.exp(-0.5 * values * values) * 0.3989422804014327
    return (values * normal_cdf, slope)


def logit_adjoint(block_result, final_gain, head_cols):
    mean_x = jnp.mean(block_result, axis=1, keepdims=True)
    centred_rows = block_result - mean_x
    inverse_deviation = lax.rsqrt(
        jnp.mean(centred_rows * centred_rows, axis=1, keepdims=True) + 1e-06
    )
    normalized_input = centred_rows * inverse_deviation
    head_scaled_rows = final_gain[:, None] * head_cols.astype(jnp.float32)
    head_average = jnp.mean(head_scaled_rows, axis=0)
    project_rows = (
        jnp.dot(normalized_input, head_scaled_rows, precision=lax.Precision.HIGHEST)
        / block_result.shape[1]
    )
    return inverse_deviation[:, :, None] * (
        head_scaled_rows.T[None, :, :]
        - head_average[None, :, None]
        - normalized_input[:, None, :] * project_rows[:, :, None]
    )


def apply_inverse(block, inverse):
    return lax.dot_general(
        block, inverse, (((1,), (1,)), ((), ())), preferred_element_type=jnp.float32
    )


def solve_panel(block, inverse):
    solved = apply_inverse(block, inverse).astype(jnp.bfloat16)
    return from_root(solved, "tensor", 0)


def body(
    normed,
    residual_in,
    w_up,
    w_down,
    final_gain,
    head_cols,
    sub_inputs,
    sub_hidden,
    panels,
    inverses,
):
    images = normed.shape[0]
    width = normed.shape[1]
    hidden_dev = w_up.shape[1]
    logits = head_cols.shape[1]
    panel = inverses.shape[1]
    rows_dev = sub_inputs.shape[0]
    tensor_rank = lax.axis_index("tensor")
    up_pre = jnp.dot(
        normed, lax.all_gather(w_up, "dp", axis=0, tiled=True), preferred_element_type=jnp.float32
    )
    activ, slope = gelu_parts(up_pre)
    hidden = activ.astype(jnp.bfloat16)
    down_full = lax.all_gather(w_down, "dp", axis=1, tiled=True)
    partial_out = jnp.dot(hidden, down_full, preferred_element_type=jnp.float32)
    block_result = residual_in.astype(jnp.float32) + lax.psum(partial_out, "tensor")
    adjoint = logit_adjoint(block_result, final_gain, head_cols).astype(jnp.bfloat16)
    back = lax.dot_general(
        adjoint.reshape(images * logits, width),
        down_full,
        (((1,), (1,)), ((), ())),
        preferred_element_type=jnp.float32,
    )
    delta = back.reshape(images, logits, hidden_dev) * slope[:, None, :]
    local_hidden = sub_hidden - tensor_rank * hidden_dev
    picked = jnp.take(normed, sub_inputs, axis=1).astype(jnp.float32)
    jac = (picked[:, None, :] * jnp.take(delta, local_hidden, axis=2)).astype(jnp.bfloat16)
    jac = jac.reshape(images * logits, rows_dev)
    first = solve_panel(jac[:, :panel], inverses[0])
    gathered = lax.all_gather(panels, "dp", axis=1, tiled=True)
    carry = jnp.dot(first, gathered[0], preferred_element_type=jnp.float32)
    second_in = (
        jac[:, panel : 2 * panel].astype(jnp.float32) - carry[:, panel : 2 * panel]
    ).astype(jnp.bfloat16)
    second = solve_panel(second_in, inverses[1])
    update = carry + jnp.dot(second, gathered[1], preferred_element_type=jnp.float32)
    below = (jac.astype(jnp.float32) - update).astype(jnp.bfloat16)
    solved_rows = jnp.concatenate([first, second, below[:, 2 * panel :]], axis=1)
    result = jnp.where(tensor_rank == 0, solved_rows, below)
    return result.reshape(images, logits, rows_dev)


def solution(mesh):
    in_specs = (
        P("dp", None),
        P("dp", None),
        P("dp", "tensor"),
        P("tensor", "dp"),
        P(),
        P(),
        P("tensor"),
        P("tensor"),
        P(None, "dp", "tensor"),
        P(),
    )
    out_specs = P("dp", None, "tensor")
    return jax.shard_map(body, mesh=mesh, in_specs=in_specs, out_specs=out_specs, check_vma=False)
```

profile of v0, /device:TPU:0, one launch (start us, length us, event | category | flops | bytes accessed | tf_op | source)
XLA Modules:
  0.0 350.0 jit_solution(9312022529404909381)
XLA Ops:
  6.5 0.7 all-gather.4.cloned.1.call-update
  7.3 0.7 all-gather.6.cloned.1.call-update
  8.1 101.4 %all-gather.4.cloned.1.call-done = bf16[1280,2560]{1,0:T(8,128)(2,1)} async-done(((bf16[80,2560]{1,0:T(8,128)(2,1)}), bf16[1280,2560]{1,0:T(8,128)(2,1)}) %all-gather.4.cloned.1.call-update) | async-done | bytes 6553616 | tf_op jit(solution)/shard_map/all_gather | solution.py:69
  109.5 4.3 %fusion.13 = (f32[64,2560]{1,0:T(8,128)S(1)}, f32[64,2560]{1,0:T(8,128)S(1)}) fusion(bf16[64,1280]{1,0:T(8,128)(2,1)} %param.10, bf16[1280,2560]{1,0:T(8,128)(2,1)} %all-gather.4.cloned.1.call-done), kind=kOutput, calls=%fused_computation.25 | convolution fusion | flops 420741120 | bytes 8028160 | tf_op jit(solution)/shard_map/dot_general | solution.py:68
  113.9 93.3 %all-gather.6.cloned.1.call-done = bf16[2560,1280]{0,1:T(8,128)(2,1)} async-done(((bf16[2560,80]{0,1:T(8,128)(2,1)}), bf16[2560,1280]{0,1:T(8,128)(2,1)}) %all-gather.6.cloned.1.call-update) | async-done | bytes 6553616 | tf_op jit(solution)/shard_map/all_gather | solution.py:73
  207.1 5.7 %fusion.18 = f32[64,1280]{1,0:T(8,128)} fusion(bf16[2560,1280]{0,1:T(8,128)(2,1)} %all-gather.6.cloned.1.call-done, f32[64,2560]{1,0:T(8,128)S(1)} %get-tuple-element.6), kind=kOutput, calls=%fused_computation.34 | convolution fusion | flops 420249600 | bytes 7536640 | tf_op jit(solution)/shard_map/dot_general | solution.py:74
  212.9 0.5 all-gather.8.cloned.1.call-update
  213.6 0.2 copy.13
  213.8 0.1 fusion.24
  214.0 0.1 subtract_bitcast_fusion
  214.0 3.2 gather_fusion
  217.3 0.2 convert_bitcast_fusion
  217.5 0.2 copy.14
  217.7 12.0 %all-reduce.4.cloned.1.call-done = f32[64,1280]{1,0:T(8,128)} async-done(((f32[64,1280]{1,0:T(8,128)}), f32[64,1280]{1,0:T(8,128)}) %all-reduce.4.cloned.1.call-update) | async-done | bytes 327696 | tf_op jit(solution)/shard_map/psum | solution.py:75
  229.6 1.1 fusion.23
  230.7 1.2 multiply_reduce_fusion
  231.9 1.1 subtract_multiply_fusion
  233.0 0.4 convolution_multiply_fusion.1
  233.4 11.7 %convolution_multiply_fusion = f32[64,16,2560]{2,1,0:T(8,128)} fusion(bf16[2560,1280]{0,1:T(8,128)(2,1)} %all-gather.6.cloned.1.call-done, f32[64,2560]{1,0:T(8,128)S(1)} %get-tuple-element.5, f32[64,16]{1,0:T(8,128)S(1)} %convolution_multiply_fusion.1, f32[64,1280]{1,0:T(8,128)S(1)} %subtract_multiply_fusion, f32[16,1280]{1,0:T(8,128)S(1)} %subtract_bitcast_fusion, ...), kind=kOutput, calls=%fused_computation.2 | convolution fusion | flops 6718750720 | bytes 18108672 | tf_op jit(solution)/shard_map/dot_general | solution.py:77
  245.1 18.9 %copy.15 = f32[64,16,2560]{0,1,2:T(8,128)} copy(f32[64,16,2560]{2,1,0:T(8,128)} %convolution_multiply_fusion) | data formatting | bytes 20971520 | tf_op jit(solution)/shard_map/mul | solution.py:83
  264.0 16.7 %gather_fusion.1 = f32[1024,64,16]{1,2,0:T(8,128)} fusion(f32[64,16,2560]{0,1,2:T(8,128)} %copy.15, s32[1024]{0:T(1024)S(1)} %fusion.27), kind=kCustom, calls=%fused_computation.1 | custom fusion | bytes 8392704 | tf_op jit(solution)/shard_map/jit(_take)/gather | solution.py:86
  280.7 7.7 %copy.16 = f32[64,16,1024]{2,1,0:T(8,128)} copy(f32[64,16,1024]{0,1,2:T(8,128)} %bitcast.35) | data formatting | bytes 8388608 | tf_op jit(solution)/shard_map/jit(_take)/gather | solution.py:86
  288.3 2.9 fusion.2
  291.3 1.1 fusion.7
  292.5 20.0 %all-reduce.6.cloned.1.call-done = bf16[1024,256]{1,0:T(8,128)(2,1)} async-done(((bf16[1024,256]{1,0:T(8,128)(2,1)}), bf16[1024,256]{1,0:T(8,128)(2,1)}) %all-reduce.6.cloned.1.call-update) | async-done | bytes 524304 | tf_op jit(solution)/shard_map/psum | solution.py:9
  312.5 1.9 fusion.15
  314.4 1.9 copy-done
  316.4 1.1 fusion.8
  317.6 20.0 %all-reduce.8.cloned.1.call-done = bf16[1024,256]{1,0:T(8,128)(2,1)} async-done(((bf16[1024,256]{1,0:T(8,128)(2,1)}), bf16[1024,256]{1,0:T(8,128)(2,1)}) %all-reduce.8.cloned.1.call-update) | async-done | bytes 524304 | tf_op jit(solution)/shard_map/psum | solution.py:9
  337.6 3.3 subtract_convert_fusion
  340.9 0.1 slice.41
  341.0 2.1 maximum_select_fusion
  (36 shorter events, 0.4 us)
Async XLA Ops:
  6.5 102.9 %all-gather.4.cloned.1.call-start = ((), (), s32[]{:S(2)}) async-start(), calls=%async_computation | async-start | bytes 6963200 | tf_op jit(solution)/shard_map/all_gather | solution.py:69
  7.3 199.9 %all-gather.6.cloned.1.call-start = ((), (), s32[]{:S(2)}) async-start(), calls=%async_computation.1 | async-start | bytes 6963200 | tf_op jit(solution)/shard_map/all_gather | solution.py:73
  8.0 221.6 %all-reduce.4.cloned.1.call-start = ((), (), s32[]{:S(2)}) async-start(), calls=%async_computation.2 | async-start | bytes 655360 | tf_op jit(solution)/shard_map/psum | solution.py:75
  113.8 99.7 %copy-start.9 = (s32[1024]{0:T(1024)S(1)}, s32[1024]{0:T(1024)}, u32[]{:S(2)}) copy-start(s32[1024]{0:T(1024)} %param.17) | copy-start | bytes 12292
  113.8 99.7 %copy-start.4 = (bf16[64,1280]{1,0:T(8,128)(2,1)S(1)}, bf16[64,1280]{1,0:T(8,128)(2,1)}, u32[]{:S(2)}) copy-start(bf16[64,1280]{1,0:T(8,128)(2,1)} %param.10) | copy-start | bytes 491524
  207.1 6.6 %copy-start.8 = (s32[1024]{0:T(1024)S(1)}, s32[1024]{0:T(1024)}, u32[]{:S(2)}) copy-start(s32[1024]{0:T(1024)} %param.16) | copy-start | bytes 12292
  207.1 6.7 %copy-start.5 = (bf16[1280,16]{0,1:T(8,128)(2,1)S(1)}, bf16[1280,16]{0,1:T(8,128)(2,1)}, u32[]{:S(2)}) copy-start(bf16[1280,16]{0,1:T(8,128)(2,1)} %param.15) | copy-start | bytes 122884
  207.1 6.7 %copy-start.6 = (f32[1280]{0:T(1024)S(1)}, f32[1280]{0:T(1024)}, u32[]{:S(2)}) copy-start(f32[1280]{0:T(1024)} %param.14) | copy-start | bytes 15364
  207.1 22.5 %copy-start.3 = (bf16[64,1280]{1,0:T(8,128)(2,1)S(1)}, bf16[64,1280]{1,0:T(8,128)(2,1)}, u32[]{:S(2)}) copy-start(bf16[64,1280]{1,0:T(8,128)(2,1)} %param.11) | copy-start | bytes 491524
  212.9 79.6 %all-gather.8.cloned.1.call-start = ((), (), s32[]{:S(2)}) async-start(), calls=%async_computation.4 | async-start | bytes 1114112 | tf_op jit(solution)/shard_map/all_gather | solution.py:89
  213.5 99.1 %all-reduce.6.cloned.1.call-start = ((), (), s32[]{:S(2)}) async-start(), calls=%async_computation.3 | async-start | bytes 1048576 | tf_op jit(solution)/shard_map/psum | solution.py:9
  288.3 2.9 copy-start.7
  292.4 45.2 %all-reduce.8.cloned.1.call-start = ((), (), s32[]{:S(2)}) async-start(), calls=%async_computation.5 | async-start | bytes 1048576 | tf_op jit(solution)/shard_map/psum | solution.py:9
  314.4 2.0 copy-start
  317.5 23.5 %copy-start.1 = (bf16[1024,256]{1,0:T(8,128)(2,1)S(1)}, bf16[1024,256]{1,0:T(8,128)(2,1)}, u32[]{:S(2)}) copy-start(bf16[1024,256]{1,0:T(8,128)(2,1)} %all-reduce.6.cloned.1.call-done) | copy-start | bytes 1572868
  337.6 3.4 copy-start.2
Sparse Core Ops, SparseCore 0:
  10.0 99.3 all-gather.3
  112.2 94.9 all-gather.5
  213.0 16.5 all-reduce.3
  232.6 56.5 all-gather.7
  292.6 19.9 all-reduce.5
  317.7 19.8 all-reduce.7
where the time goes:
time: 351 us; the launch traced here: 350 us
  waiting for transfers between devices  249 us (71%)
  local copies, waits for them, and re-layouts  48.9 us (14%)
  matrix products  29.6 us (8%)
  between operations  13.7 us (4%)
  other arithmetic  8.85 us (3%)
    all_gather x1, waiting for transfers between devices, body(): lax.all_gather(w_up, 'dp', axis=0, tiled=True)  101 us
    all_gather x1, waiting for transfers between devices, body(): down_full = lax.all_gather(w_down, 'dp', axis=1, tiled=True)  93.3 us
    psum x2, waiting for transfers between devices, from_root(): return lax.psum(jnp.where(mine, shard, jnp.zeros_like(shard)), axis)  40 us
    gather x2, local copies, waits for them, and re-layouts, body(): jnp.take(delta, local_hidden, axis=2)  24.3 us
    mul x1, local copies, waits for them, and re-layouts, body(): delta = back.reshape(images, logits, hidden_dev) * slope[:, None, :]  18.9 us
    psum x1, waiting for transfers between devices, body(): lax.psum(partial_out, 'tensor')  12 us
    dot_general x1, matrix products, body(): lax.dot_general(adjoint.reshape(images * logits, width), down_full, (((1,...  11.7 us
  transfers between devices with their start and end apart: 6, of which 5 were waited for; matrix products, arithmetic and copies ran while one was open for 20% of the time, Pallas kernels for 0%

commit v1 on v0

v1 whole, which is shorter than its diff:
```python
import functools

import jax
import jax.numpy as jnp
from jax import lax
from jax.experimental import pallas as pl
from jax.experimental.pallas import tpu as pltpu
from jax.sharding import PartitionSpec as P

MESH = pl.DeviceIdType.MESH
GROUP = 4
F32 = jnp.float32
BF16 = jnp.bfloat16


def gelu_parts(values):
    normal_cdf = 0.5 * (1.0 + lax.erf(values * 0.7071067811865476))
    slope = normal_cdf + values * jnp.exp(-0.5 * values * values) * 0.3989422804014327
    return (values * normal_cdf, slope)


def normalize(block_result):
    mean_x = jnp.mean(block_result, axis=1, keepdims=True)
    centred = block_result - mean_x
    inv_std = lax.rsqrt(jnp.mean(centred * centred, axis=1, keepdims=True) + 1e-06)
    return centred * inv_std, inv_std


def front_kernel(
    planes,
    pairs,
    normed_ref, resid_ref, wup_ref, wdt_ref, head_ref,
    side_ref, back_ref, xhat_ref, istd_ref,
    nall, wu, wd, part, parts_in, pair_out, pair_in, xown, xall,
    side_src, side_in, back_src, back_in,
    local_sem, flat_send, flat_recv, up_send, up_recv, dn_send, dn_recv, pair_send, pair_recv,
):
    d = lax.axis_index("dp")
    t = lax.axis_index("tensor")
    z = d // GROUP
    p = lax.rem(d, GROUP)
    images, width = normed_ref.shape
    cols = wu.shape[3]
    logits = head_ref.shape[0] // 2
    last = planes - 1
    others = range(1, GROUP)

    barrier = pltpu.get_barrier_semaphore()
    for o in others:
        pl.semaphore_signal(barrier, inc=1, device_id=(z * GROUP + (p ^ o), t), device_id_type=MESH)
    pl.semaphore_signal(barrier, inc=1, device_id=(d, 1 - t), device_id_type=MESH)

    @pl.when(z > 0)
    def _():
        pl.semaphore_signal(barrier, inc=1, device_id=(d - GROUP, t), device_id_type=MESH)

    @pl.when(z < last)
    def _():
        pl.semaphore_signal(barrier, inc=1, device_id=(d + GROUP, t), device_id_type=MESH)

    pl.semaphore_wait(barrier, GROUP + jnp.where(z > 0, 1, 0) + jnp.where(z < last, 1, 0))

    def flat(src, dst, kind, o):
        return pltpu.make_async_remote_copy(
            src_ref=src, dst_ref=dst, send_sem=flat_send.at[kind, o], recv_sem=flat_recv.at[kind, o],
            device_id=(z * GROUP + (p ^ o), t), device_id_type=MESH,
        )

    def block(ref, q):
        return ref.at[:, pl.ds(pl.multiple_of(q * cols, 128), cols)]

    sent = []
    own = [
        pltpu.make_async_copy(block(wup_ref, p), wu.at[z, p], local_sem.at[0]),
        pltpu.make_async_copy(block(wdt_ref, p), wd.at[z, p], local_sem.at[1]),
        pltpu.make_async_copy(normed_ref, nall.at[p], local_sem.at[2]),
    ]
    for copy in own:
        copy.start()
    moves = {}
    for kind in (0, 1, 2):
        for o in others:
            if kind == 0:
                copy = flat(block(wup_ref, p ^ o), wu.at[z, p], 0, o)
            elif kind == 1:
                copy = flat(block(wdt_ref, p ^ o), wd.at[z, p], 1, o)
            else:
                copy = flat(normed_ref, nall.at[p], 2, o)
            copy.start()
            moves[kind, o] = copy
            sent.append(copy)

    def hop(buf, w, src, s, step):
        send, recv = (up_send, up_recv) if step > 0 else (dn_send, dn_recv)
        return pltpu.make_async_remote_copy(
            src_ref=buf.at[src], dst_ref=buf.at[src], send_sem=send.at[w, s], recv_sem=recv.at[w, s],
            device_id=(d + step * GROUP, t), device_id_type=MESH,
        )

    def relay(buf, w, s):
        @pl.when(z >= s)
        def _():
            if s > 0:
                hop(buf, w, z - s, s - 1, 1).wait_recv()

            @pl.when(z < last)
            def _():
                hop(buf, w, z - s, s, 1).start()

        @pl.when(z + s <= last)
        def _():
            if s > 0:
                hop(buf, w, z + s, s - 1, -1).wait_recv()

            @pl.when(z > 0)
            def _():
                hop(buf, w, z + s, s, -1).start()

    for w, buf in enumerate((wu, wd)):
        own[w].wait()
        for o in others:
            moves[w, o].wait_recv()
        relay(buf, w, 0)
    own[2].wait()
    for o in others:
        moves[2, o].wait_recv()
    for s in range(1, planes):
        relay(wu, 0, s)

    rows = GROUP * images
    up_pre = jnp.dot(
        nall[...].reshape(rows, width), wu[...].reshape(width, cols), preferred_element_type=F32
    )
    activ, slope = gelu_parts(up_pre)
    hidden = activ.astype(BF16)
    side_src[:, :images, :] = slope.reshape(GROUP, images, cols)

    for s in range(1, planes):
        relay(wd, 1, s)
    down = wd[...].reshape(width, cols)
    partial = lax.dot_general(hidden, down, (((1,), (1,)), ((), ())), preferred_element_type=F32)
    pair_out[...] = partial.reshape(GROUP, images, width)
    part[...] = partial.astype(BF16).reshape(GROUP, images, width)
    for o in others:
        copy = flat(part.at[p ^ o], parts_in.at[o - 1], 3, o)
        copy.start()
        moves[3, o] = copy
        sent.append(copy)
    head_back = jnp.dot(head_ref[...], down, preferred_element_type=F32)
    head_back = head_back[:logits] + head_back[logits:]
    for q in range(GROUP):
        side_src[q, images:, :] = head_back
    total = pair_out[p]
    for o in others:
        moves[3, o].wait_recv()
        total = total + parts_in[o - 1].astype(F32)
    xhat_ref[...] = total
    swap = pltpu.make_async_remote_copy(
        src_ref=xhat_ref, dst_ref=pair_in, send_sem=pair_send, recv_sem=pair_recv,
        device_id=(d, 1 - t), device_id_type=MESH,
    )
    swap.start()
    swap.wait()
    block_out = resid_ref[...].astype(F32) + (xhat_ref[...] + pair_in[...])
    xhat, inv_std = normalize(block_out)
    xown[...] = xhat.astype(BF16)
    for o in others:
        copy = flat(xown, xall.at[p], 4, o)
        copy.start()
        moves[4, o] = copy
        sent.append(copy)
    xall[p] = xown[...]
    xhat_ref[...] = xhat
    istd_ref[...] = jnp.broadcast_to(inv_std, istd_ref.shape)
    for o in others:
        copy = flat(side_src.at[p ^ o], side_in.at[p], 5, o)
        copy.start()
        moves[5, o] = copy
        sent.append(copy)
    side_in[p] = side_src[p]
    for o in others:
        moves[4, o].wait_recv()
    back = jnp.dot(xall[...].reshape(rows, width), down, preferred_element_type=F32)
    back_src[...] = back.reshape(GROUP, images, cols)
    for o in others:
        copy = flat(back_src.at[p ^ o], back_in.at[p], 6, o)
        copy.start()
        moves[6, o] = copy
        sent.append(copy)
    back_in[p] = back_src[p]
    for kind in (5, 6):
        for o in others:
            moves[kind, o].wait_recv()
    for q in range(GROUP):
        side_ref[:, q * cols : (q + 1) * cols] = side_in[q]
        back_ref[:, q * cols : (q + 1) * cols] = back_in[q]
    for copy in sent:
        copy.wait_send()
    for w, buf in enumerate((wu, wd)):
        for s in range(planes):
            @pl.when((z >= s) & (z < last))
            def _():
                hop(buf, w, z - s, s, 1).wait_send()

            @pl.when((z + s <= last) & (z > 0))
            def _():
                hop(buf, w, z + s, s, -1).wait_send()


def fused_front(normed, residual_in, w_up, w_down, head_pair, members):
    images, width = normed.shape
    depth, hidden_dev = w_up.shape
    logits = head_pair.shape[0] // 2
    planes = members // GROUP
    cols = hidden_dev // GROUP
    side = images + logits
    dma = pltpu.SemaphoreType.DMA
    vmem = pl.BlockSpec(memory_space=pltpu.VMEM)
    return pl.pallas_call(
        functools.partial(front_kernel, planes, 2),
        out_shape=(
            jax.ShapeDtypeStruct((side, hidden_dev), F32),
            jax.ShapeDtypeStruct((images, hidden_dev), F32),
            jax.ShapeDtypeStruct((images, width), F32),
            jax.ShapeDtypeStruct((images, 128), F32),
        ),
        in_specs=[vmem] * 5,
        out_specs=(vmem,) * 4,
        scratch_shapes=[
            pltpu.VMEM((GROUP, images, width), BF16),
            pltpu.VMEM((planes, GROUP, depth, cols), BF16),
            pltpu.VMEM((planes, GROUP, depth, cols), BF16),
            pltpu.VMEM((GROUP, images, width), BF16),
            pltpu.VMEM((GROUP - 1, images, width), BF16),
            pltpu.VMEM((GROUP, images, width), F32),
            pltpu.VMEM((images, width), F32),
            pltpu.VMEM((images, width), BF16),
            pltpu.VMEM((GROUP, images, width), BF16),
            pltpu.VMEM((GROUP, side, cols), F32),
            pltpu.VMEM((GROUP, side, cols), F32),
            pltpu.VMEM((GROUP, images, cols), F32),
            pltpu.VMEM((GROUP, images, cols), F32),
            dma((3,)),
            dma((7, GROUP)),
            dma((7, GROUP)),
            dma((2, planes)),
            dma((2, planes)),
            dma((2, planes)),
            dma((2, planes)),
            dma,
            dma,
        ],
        compiler_params=pltpu.CompilerParams(
            collective_id=0, has_side_effects=True, vmem_limit_bytes=40 * 1024 * 1024
        ),
        cost_estimate=pl.CostEstimate(
            flops=8 * images * width * hidden_dev,
            bytes_accessed=40 * depth * hidden_dev,
            transcendentals=2 * images * hidden_dev,
        ),
    )(normed, residual_in, w_up, w_down.T, head_pair)


def plain_front(normed, residual_in, w_up, w_down, head_pair):
    images = normed.shape[0]
    logits = head_pair.shape[0] // 2
    up_pre = jnp.dot(
        normed, lax.all_gather(w_up, "dp", axis=0, tiled=True), preferred_element_type=F32
    )
    activ, slope = gelu_parts(up_pre)
    down_full = lax.all_gather(w_down, "dp", axis=1, tiled=True)
    partial_out = jnp.dot(activ.astype(BF16), down_full, preferred_element_type=F32)
    block_out = residual_in.astype(F32) + lax.psum(partial_out, "tensor")
    xhat, inv_std = normalize(block_out)
    both = jnp.concatenate([head_pair, xhat.astype(BF16)], axis=0)
    out = lax.dot_general(both, down_full, (((1,), (1,)), ((), ())), preferred_element_type=F32)
    head_back = out[:logits] + out[logits : 2 * logits]
    return jnp.concatenate([slope, head_back], axis=0), out[2 * logits :], xhat, inv_std


def from_first(value, ranks, tensor_rank):
    if ranks == 2:
        other = lax.ppermute(value, "tensor", [(0, 1)])
        return jnp.where(tensor_rank == 0, value, other)
    return lax.psum(jnp.where(tensor_rank == 0, value, jnp.zeros_like(value)), "tensor")


def body(
    members,
    ranks,
    normed,
    residual_in,
    w_up,
    w_down,
    final_gain,
    head_cols,
    sub_inputs,
    sub_hidden,
    panels,
    inverses,
):
    images, width = normed.shape
    hidden_dev = w_up.shape[1]
    logits = head_cols.shape[1]
    panel = inverses.shape[1]
    rows_dev = sub_inputs.shape[0]
    tensor_rank = lax.axis_index("tensor")

    corner = from_first(panels[0, :, panel : 2 * panel], ranks, tensor_rank)
    joined = jnp.concatenate([panels[0], panels[1], corner], axis=1)
    gathered = lax.all_gather(joined, "dp", axis=0, tiled=True)

    scaled_head = (final_gain[:, None] * head_cols.astype(F32)).T
    centred_head = scaled_head - jnp.mean(scaled_head, axis=1, keepdims=True)
    head_high = centred_head.astype(BF16)
    head_low = (centred_head - head_high.astype(F32)).astype(BF16)
    head_pair = jnp.concatenate([head_high, head_low], axis=0)

    fits = (
        ranks == 2
        and members % GROUP == 0
        and hidden_dev % (GROUP * 128) == 0
        and w_up.shape[0] % 16 == 0
        and images % 16 == 0
    )
    if fits:
        side, back, xhat, inv_std = fused_front(
            normed, residual_in, w_up, w_down, head_pair, members
        )
    else:
        side, back, xhat, inv_std = plain_front(normed, residual_in, w_up, w_down, head_pair)
    inv_std = inv_std[:, :1]
    project = (
        lax.dot_general(
            xhat, scaled_head, (((1,), (1,)), ((), ())), precision=lax.Precision.HIGHEST
        )
        / width
    )
    picked = jnp.take(normed, sub_inputs, axis=1).astype(F32)
    local_hidden = sub_hidden - tensor_rank * hidden_dev
    chosen = jnp.take(jnp.concatenate([side, back], axis=0), local_hidden, axis=1)
    gain = chosen[:images] * picked * inv_std
    head_back = chosen[images : images + logits]
    bent = chosen[images + logits :]

    def jacobian(gain, head_back, bent):
        return (
            gain[:, None, :] * (head_back[None, :, :] - project[:, :, None] * bent[:, None, :])
        ).astype(BF16).reshape(images * logits, gain.shape[1])

    packed = jnp.concatenate([gain, head_back, bent], axis=0)[:, : 2 * panel]
    packed = from_first(packed, ranks, tensor_rank)
    top = jacobian(packed[:images], packed[images : images + logits], packed[images + logits :])
    jac = jacobian(gain, head_back, bent)

    def solve(block, inverse):
        return lax.dot_general(
            block, inverse, (((1,), (1,)), ((), ())), preferred_element_type=F32
        ).astype(BF16)

    first = solve(top[:, :panel], inverses[0])
    second_in = top[:, panel:].astype(F32) - jnp.dot(
        first, gathered[:, 2 * rows_dev :], preferred_element_type=F32
    )
    second = solve(second_in.astype(BF16), inverses[1])
    solved = jnp.concatenate([first, second], axis=1)
    lower = jnp.concatenate([gathered[:, :rows_dev], gathered[:, rows_dev : 2 * rows_dev]], axis=0)
    update = jnp.dot(solved, lower, preferred_element_type=F32)
    below = (jac.astype(F32) - update).astype(BF16)
    head_part = jnp.where(tensor_rank == 0, solved, below[:, : 2 * panel])
    result = jnp.concatenate([head_part, below[:, 2 * panel :]], axis=1)
    return result.reshape(images, logits, rows_dev)


def solution(mesh):
    in_specs = (
        P("dp", None),
        P("dp", None),
        P("dp", "tensor"),
        P("tensor", "dp"),
        P(),
        P(),
        P("tensor"),
        P("tensor"),
        P(None, "dp", "tensor"),
        P(),
    )
    out_specs = P("dp", None, "tensor")
    return jax.shard_map(
        functools.partial(body, mesh.shape["dp"], mesh.shape["tensor"]),
        mesh=mesh, in_specs=in_specs, out_specs=out_specs, check_vma=False,
    )
```

time: 351 us -> 200 us (0.57)
  waiting for transfers between devices: 249 us -> 19.6 us
  Pallas kernels: 0 us -> 98.1 us
  matrix products: 29.6 us -> 8.43 us
  starting transfers between devices: 0.2 us -> 4.86 us
    all_gather x3 -> x1, waiting for transfers between devices: 195 us -> 19.5 us  [body(): gathered = lax.all_gather(joined, 'dp', axis=0, tiled=True)]
    pallas_call x0 -> x1, Pallas kernels: none -> 98.1 us  [fused_front(): pl.pallas_call(functools.partial(front_kernel, planes, 2), out_shape=(jax...]
    psum x3 -> x0, waiting for transfers between devices: 52 us -> none  [the longest x2 40 us: from_root(): return lax.psum(jnp.where(mine, shard, jnp.zeros_like(shard)), axis)]
    dot_general x8 -> x4, matrix products: 29.6 us -> 8.43 us  [the longest x1 6.23 us: body(): update = jnp.dot(solved, lower, preferred_element_type=F32)]
    gather x3 -> x2, local copies, waits for them, and re-layouts: 27.5 us -> 7.88 us  [the longest x1 4.68 us: body(): jnp.take(jnp.concatenate([side, back], axis=0), local_hidden, axis=1)]
    sub x0 -> x2, local copies, waits for them, and re-layouts: none -> 7.93 us  [jacobian(): head_back[None, :, :] - project[:, :, None] * bent[:, None, :]]
    ppermute x0 -> x2, starting transfers between devices: none -> 4.86 us  [from_first(): other = lax.ppermute(value, 'tensor', [(0, 1)])]
    concatenate x0 -> x2, local copies, waits for them, and re-layouts: none -> 4.52 us  [the longest x1 2.56 us: body(): result = jnp.concatenate([head_part, below[:, 2 * panel:]], axis=1)]
  transfers between devices with their start and end apart: 6 -> 3, of which waited for: 5 -> 1; matrix products, arithmetic and copies ran while one was open for 20% -> 22% of each run, Pallas kernels for 0% -> 49%
where the time goes in v1:
time: 200 us; the launch traced here: 199 us
  Pallas kernels  98.1 us (49%)
  local copies, waits for them, and re-layouts  46.1 us (23%)
  waiting for transfers between devices  19.6 us (10%)
  between operations  13.6 us (7%)
  matrix products  8.43 us (4%)
  other arithmetic  8.33 us (4%)
  starting transfers between devices  4.86 us (2%)
    pallas_call x1, Pallas kernels, fused_front(): pl.pallas_call(functools.partial(front_kernel, planes, 2), out_shape=(jax...  98.1 us
    all_gather x1, waiting for transfers between devices, body(): gathered = lax.all_gather(joined, 'dp', axis=0, tiled=True)  19.5 us
    mul x3, local copies, waits for them, and re-layouts, jacobian(): project[:, :, None] * bent[:, None, :]  7.98 us
    sub x2, local copies, waits for them, and re-layouts, jacobian(): head_back[None, :, :] - project[:, :, None] * bent[:, None, :]  7.93 us
    mul x2, local copies, waits for them, and re-layouts, jacobian(): gain[:, None, :]  7.89 us
    dot_general x1, matrix products, body(): update = jnp.dot(solved, lower, preferred_element_type=F32)  6.23 us
    ppermute x2, starting transfers between devices, from_first(): other = lax.ppermute(value, 'tensor', [(0, 1)])  4.86 us
    gather x1, local copies, waits for them, and re-layouts, body(): jnp.take(jnp.concatenate([side, back], axis=0), local_hidden, axis=1)  4.68 us
  transfers between devices with their start and end apart: 3, of which 1 were waited for; matrix products, arithmetic and copies ran while one was open for 22% of the time, Pallas kernels for 49%

profile of v1, /device:TPU:0, one launch (start us, length us, event | category | flops | bytes accessed | tf_op | source)
XLA Modules:
  0.0 199.0 jit_solution(10712864909924475960)
XLA Ops:
  6.5 0.7 slice_bitcast_fusion.2
  7.2 2.3 %collective-permute-start.1 = (bf16[16,256]{1,0:T(8,128)(2,1)S(1)}, bf16[16,256]{1,0:T(8,128)(2,1)S(1)}, u32[]{:S(2)}, u32[]{:S(2)}) collective-permute-start(bf16[16,256]{1,0:T(8,128)(2,1)S(1)} %slice_bitcast_fusion.2), channel_id=1, source_target_pairs={{0,1},{2,3},{4,5},{6,7},{8,9},{10,11},{12,13},{14,15},{16,17},{18,... | collective-permute-start | bytes 24584 | tf_op jit(solution)/shard_map/ppermute | solution.py:283
  9.6 0.9 fusion.19
  10.5 0.9 fusion.17
  11.4 0.9 bitcast_convert_fusion
  12.2 0.8 slice_bitcast_fusion.1
  13.0 0.9 copy-done
  13.9 1.0 copy-done.2
  14.9 1.0 copy-done.3
  15.9 0.9 copy-done.4
  16.9 98.1 %shard_map.100 = (f32[80,2560]{1,0:T(8,128)S(1)}, f32[64,2560]{1,0:T(8,128)S(1)}, f32[64,1280]{1,0:T(8,128)S(1)}, f32[64,128]{1,0:T(8,128)S(1)}) custom-call(bf16[64,1280]{1,0:T(8,128)(2,1)S(1)} %copy-done, bf16[64,1280]{1,0:T(8,128)(2,1)S(1)} %copy-done.4, bf16[80,2560]{1,0:T(8,128)(2,1)S(1)} %copy-done.2, bf16[80,2560]{1,0:T(8,128)(2,1)S(1)} %bitcast.44, ...), custom_call_target="tpu_custom_call" | custom-call | flops 1677721600 | bytes 8192000 | tf_op jit(solution)/shard_map/pallas_call | solution.py:219
  115.0 1.2 pad_maximum_fusion.1
  116.4 2.0 copy.17
  118.4 4.7 %gather_fusion = f32[1024,144]{1,0:T(8,128)} fusion(f32[144,2560]{0,1:T(8,128)S(1)} %copy.17, s32[1024]{0:T(1024)S(1)} %fusion.22), kind=kCustom, calls=%fused_computation | custom fusion | bytes 1183744 | tf_op jit(solution)/shard_map/jit(_take)/gather | solution.py:341
  123.1 0.7 broadcast_select_fusion.1
  123.8 0.6 pad_maximum_fusion.6
  124.5 1.4 select_bitcast_fusion
  125.9 1.0 slice.89
  126.9 3.2 %gather_fusion.1 = bf16[1024,64]{1,0:T(8,128)(2,1)S(1)} fusion(bf16[64,1280]{0,1:T(8,128)(2,1)S(1)} %copy.18, s32[1024]{0:T(1024)S(1)} %fusion.21), kind=kCustom, calls=%fused_computation.1 | custom fusion | bytes 266240 | tf_op jit(solution)/shard_map/jit(_take)/gather | solution.py:339
  131.4 2.5 %collective-permute-start = (f32[144,512]{0,1:T(8,128)S(1)}, f32[144,512]{0,1:T(8,128)}, u32[]{:S(2)}, u32[]{:S(2)}) collective-permute-start(f32[144,512]{0,1:T(8,128)S(1)} %pad_maximum_fusion.4), channel_id=1, source_target_pairs={{0,1},{2,3},{4,5},{6,7},{8,9},{10,11},{12,13},{14,15},{16,17},{18,... | collective-permute-start | bytes 884744 | tf_op jit(solution)/shard_map/ppermute | solution.py:283
  134.3 2.5 %mul.95 = f32[64,16,1024]{2,1,0:T(8,128)} broadcast(f32[64,1024]{1,0:T(8,128)S(1)} %copy.23), dimensions={0,2} | broadcast | bytes 4456448 | tf_op jit(solution)/shard_map/mul | solution.py:348
  136.8 5.4 %copy.28 = f32[1024,1024]{0,1:T(8,128)} copy(f32[1024,1024]{1,0:T(8,128)} %bitcast.45) | data formatting | bytes 8388608 | tf_op jit(solution)/shard_map/mul | solution.py:348
  142.3 2.5 %sub.58 = f32[64,16,1024]{2,1,0:T(8,128)} broadcast(f32[16,1024]{1,0:T(8,128)S(1)} %copy.24), dimensions={1,2} | broadcast | bytes 4259840 | tf_op jit(solution)/shard_map/sub | solution.py:348
  144.8 5.4 %copy.27 = f32[1024,1024]{0,1:T(8,128)} copy(f32[1024,1024]{1,0:T(8,128)} %bitcast.46) | data formatting | bytes 8388608 | tf_op jit(solution)/shard_map/sub | solution.py:348
  150.4 2.5 %mul.98 = f32[64,16,1024]{2,1,0:T(8,128)} broadcast(f32[64,1024]{1,0:T(8,128)S(1)} %copy.25), dimensions={0,2} | broadcast | bytes 4456448 | tf_op jit(solution)/shard_map/mul | solution.py:348
  152.9 5.4 %copy.26 = f32[1024,1024]{0,1:T(8,128)} copy(f32[1024,1024]{1,0:T(8,128)} %bitcast.47) | data formatting | bytes 8388608 | tf_op jit(solution)/shard_map/mul | solution.py:348
  160.2 19.5 %all-gather.2.cloned.1.call-done = bf16[256,2304]{1,0:T(8,128)(2,1)} async-done(((bf16[16,2304]{1,0:T(8,128)(2,1)}), bf16[256,2304]{1,0:T(8,128)(2,1)}) %all-gather.2.cloned.1.call-update) | async-done | bytes 1179664 | tf_op jit(solution)/shard_map/all_gather | solution.py:311
  179.8 1.3 fusion.24
  181.1 1.5 convolution_convert_fusion
  182.6 6.2 %subtract_convert_fusion = bf16[1024,1024]{0,1:T(8,128)(2,1)S(1)} fusion(f32[1024,1024]{0,1:T(8,128)} %copy.28, f32[1024,1024]{0,1:T(8,128)} %copy.27, f32[1024,1024]{0,1:T(8,128)} %copy.26, f32[1024]{0:T(1024)S(1)} %mul.89, bf16[256,1024]{1,0:T(8,128)(2,1)S(1)} %get-tuple-element.16, bf16[256,1024]{1,0:T(8,128)(2,1)S(1)} %get-tuple-element.15, ...), kind=kOutput, calls=%fused_computation.2 | convolution fusion | flops 1085276160 | bytes 16781312 | tf_op jit(solution)/shard_map/dot_general | solution.py:368
  188.8 0.6 slice_select_fusion
  189.6 2.6 %copy.29 = bf16[1024,1024]{1,0:T(8,128)(2,1)} copy(bf16[1024,1024]{0,1:T(8,128)(2,1)S(1)} %pad_maximum_fusion) | data formatting | bytes 4194304 | tf_op jit(solution)/shard_map/concatenate | solution.py:371
  (50 shorter events, 4.3 us)
Async XLA Ops:
  6.5 173.2 %all-gather.2.cloned.1.call-start = ((), (), s32[]{:S(2)}) async-start(), calls=%async_computation | async-start | bytes 1253376 | tf_op jit(solution)/shard_map/all_gather | solution.py:311
  7.2 115.9 %collective-permute-start.1 = (bf16[16,256]{1,0:T(8,128)(2,1)S(1)}, bf16[16,256]{1,0:T(8,128)(2,1)S(1)}, u32[]{:S(2)}, u32[]{:S(2)}) collective-permute-start(bf16[16,256]{1,0:T(8,128)(2,1)S(1)} %slice_bitcast_fusion.2), channel_id=1, source_target_pairs={{0,1},{2,3},{4,5},{6,7},{8,9},{10,11},{12,13},{14,15},{16,17},{18,... | collective-permute-start | bytes 24584 | tf_op jit(solution)/shard_map/ppermute | solution.py:283
  13.0 0.9 copy-start
  13.9 1.0 copy-start.2
  14.9 1.0 copy-start.3
  15.9 0.9 copy-start.4
  114.9 1.2 copy-start.11
  115.0 1.3 copy-start.1
  123.1 3.8 %copy-start.10 = (s32[1024]{0:T(1024)S(1)}, s32[1024]{0:T(1024)}, u32[]{:S(2)}) copy-start(s32[1024]{0:T(1024)} %param.16) | copy-start | bytes 12292
  130.1 1.0 copy-start.5
  131.4 27.5 %collective-permute-start = (f32[144,512]{0,1:T(8,128)S(1)}, f32[144,512]{0,1:T(8,128)}, u32[]{:S(2)}, u32[]{:S(2)}) collective-permute-start(f32[144,512]{0,1:T(8,128)S(1)} %pad_maximum_fusion.4), channel_id=1, source_target_pairs={{0,1},{2,3},{4,5},{6,7},{8,9},{10,11},{12,13},{14,15},{16,17},{18,... | collective-permute-start | bytes 884744 | tf_op jit(solution)/shard_map/ppermute | solution.py:283
  152.9 5.4 %copy-start.6 = (bf16[1280,16]{0,1:T(8,128)(2,1)S(1)}, bf16[1280,16]{0,1:T(8,128)(2,1)}, u32[]{:S(2)}) copy-start(bf16[1280,16]{0,1:T(8,128)(2,1)} %param.15) | copy-start | bytes 122884
  152.9 5.4 %copy-start.7 = (f32[1280]{0:T(1024)S(1)}, f32[1280]{0:T(1024)}, u32[]{:S(2)}) copy-start(f32[1280]{0:T(1024)} %param.14) | copy-start | bytes 15364
  158.9 1.0 copy-start.8
  159.6 21.5 %copy-start.9 = (bf16[2,256,256]{2,1,0:T(8,128)(2,1)S(1)}, bf16[2,256,256]{2,1,0:T(8,128)(2,1)}, u32[]{:S(2)}) copy-start(bf16[2,256,256]{2,1,0:T(8,128)(2,1)} %param.19) | copy-start | bytes 786436
Sparse Core Ops, SparseCore 0:
  124.6 55.1 all-gather.1

commit v2 on v1

v2 whole, which is shorter than its diff:
```python
import functools

import jax
import jax.numpy as jnp
from jax import lax
from jax.experimental import pallas as pl
from jax.experimental.pallas import tpu as pltpu
from jax.sharding import PartitionSpec as P

MESH = pl.DeviceIdType.MESH
GROUP = 4
F32 = jnp.float32
BF16 = jnp.bfloat16


def gelu_parts(values):
    normal_cdf = 0.5 * (1.0 + lax.erf(values * 0.7071067811865476))
    slope = normal_cdf + values * jnp.exp(-0.5 * values * values) * 0.3989422804014327
    return (values * normal_cdf, slope)


def normalize(block_result):
    mean_x = jnp.mean(block_result, axis=1, keepdims=True)
    centred = block_result - mean_x
    inv_std = lax.rsqrt(jnp.mean(centred * centred, axis=1, keepdims=True) + 1e-06)
    return centred * inv_std, inv_std


def halves(values):
    high = values.astype(BF16)
    return high, (values - high.astype(F32)).astype(BF16)


def pick_columns(values, index, size):
    where = lax.broadcasted_iota(jnp.int32, (size, index.shape[1]), 0)
    chosen = jnp.where(where == index, 1.0, 0.0).astype(BF16)
    return jnp.dot(values, chosen, preferred_element_type=F32)


def front_kernel(
    planes,
    panel,
    normed_hbm, resid_hbm, wup_ref, wdt_ref, gain_ref, head_ref, inputs_ref, units_ref,
    pick_ref, top_ref, project_ref,
    normed_ref, resid_ref, nall, wu, wd, part, parts_in, pair_out, pair_in, xown, xall,
    side_src, side_in, back_src, back_in, onehot, xsum, pick_out, pick_in,
    local_sem, flat_send, flat_recv, up_send, up_recv, dn_send, dn_recv, pair_send, pair_recv,
):
    d = lax.axis_index("dp")
    t = lax.axis_index("tensor")
    z = d // GROUP
    p = lax.rem(d, GROUP)
    images, width = normed_ref.shape
    cols = wu.shape[3]
    logits = head_ref.shape[0]
    last = planes - 1
    others = range(1, GROUP)

    barrier = pltpu.get_barrier_semaphore()
    for o in others:
        pl.semaphore_signal(barrier, inc=1, device_id=(z * GROUP + (p ^ o), t), device_id_type=MESH)
    pl.semaphore_signal(barrier, inc=1, device_id=(d, 1 - t), device_id_type=MESH)

    @pl.when(z > 0)
    def _():
        pl.semaphore_signal(barrier, inc=1, device_id=(d - GROUP, t), device_id_type=MESH)

    @pl.when(z < last)
    def _():
        pl.semaphore_signal(barrier, inc=1, device_id=(d + GROUP, t), device_id_type=MESH)

    pl.semaphore_wait(barrier, GROUP + jnp.where(z > 0, 1, 0) + jnp.where(z < last, 1, 0))

    def flat(src, dst, kind, o):
        return pltpu.make_async_remote_copy(
            src_ref=src, dst_ref=dst, send_sem=flat_send.at[kind, o], recv_sem=flat_recv.at[kind, o],
            device_id=(z * GROUP + (p ^ o), t), device_id_type=MESH,
        )

    def block(ref, q):
        return ref.at[:, pl.ds(pl.multiple_of(q * cols, 128), cols)]

    sent = []
    own = [
        pltpu.make_async_copy(block(wup_ref, p), wu.at[z, p], local_sem.at[0]),
        pltpu.make_async_copy(block(wdt_ref, p), wd.at[z, p], local_sem.at[1]),
        pltpu.make_async_copy(normed_hbm, normed_ref, local_sem.at[2]),
        pltpu.make_async_copy(resid_hbm, resid_ref, local_sem.at[3]),
    ]
    moves = {}

    def spread(kind, pick, dst):
        for o in others:
            copy = flat(pick(p ^ o), dst, kind, o)
            copy.start()
            moves[kind, o] = copy
            sent.append(copy)

    def landed(kind):
        for o in others:
            moves[kind, o].wait_recv()

    spread(0, lambda q: block(wup_ref, q), wu.at[z, p])
    for copy in own:
        copy.start()
    own[2].wait()
    own[3].wait()
    nall[p] = normed_ref[...]
    head = head_ref[...].astype(F32) * gain_ref[...]
    head = head - jnp.mean(head, axis=1, keepdims=True)
    head_high, head_low = halves(head)
    head_pair = jnp.concatenate([head_high, head_low], axis=0)

    def hop(buf, w, src, s, step):
        send, recv = (up_send, up_recv) if step > 0 else (dn_send, dn_recv)
        return pltpu.make_async_remote_copy(
            src_ref=buf.at[src], dst_ref=buf.at[src], send_sem=send.at[w, s], recv_sem=recv.at[w, s],
            device_id=(d + step * GROUP, t), device_id_type=MESH,
        )

    def relay(buf, w, s):
        @pl.when(z >= s)
        def _():
            if s > 0:
                hop(buf, w, z - s, s - 1, 1).wait_recv()

            @pl.when(z < last)
            def _():
                hop(buf, w, z - s, s, 1).start()

        @pl.when(z + s <= last)
        def _():
            if s > 0:
                hop(buf, w, z + s, s - 1, -1).wait_recv()

            @pl.when(z > 0)
            def _():
                hop(buf, w, z + s, s, -1).start()

    own[0].wait()
    landed(0)
    relay(wu, 0, 0)
    spread(1, lambda q: block(wdt_ref, q), wd.at[z, p])
    own[1].wait()
    landed(1)
    relay(wd, 1, 0)
    spread(2, lambda q: normed_ref, nall.at[p])
    picked = pick_columns(normed_ref[...], inputs_ref[...], width)
    chunk = lax.broadcasted_iota(jnp.int32, (cols, units_ref.shape[1]), 0)
    relay(wu, 0, 1)
    for q in range(GROUP):
        onehot[q] = jnp.where(chunk + q * cols == units_ref[...], 1.0, 0.0).astype(BF16)
    landed(2)
    for s in range(2, planes):
        relay(wu, 0, s)

    rows = GROUP * images
    up_pre = jnp.dot(
        nall[...].reshape(rows, width), wu[...].reshape(width, cols), preferred_element_type=F32
    )
    activ, slope = gelu_parts(up_pre)
    hidden = activ.astype(BF16)
    side_src[:, :images, :] = slope.reshape(GROUP, images, cols)

    for s in range(1, planes):
        relay(wd, 1, s)
    down = wd[...].reshape(width, cols)
    partial = lax.dot_general(hidden, down, (((1,), (1,)), ((), ())), preferred_element_type=F32)
    pair_out[...] = partial.reshape(GROUP, images, width)
    part[...] = partial.astype(BF16).reshape(GROUP, images, width)
    for o in others:
        copy = flat(part.at[p ^ o], parts_in.at[o - 1], 3, o)
        copy.start()
        moves[3, o] = copy
        sent.append(copy)
    head_back = jnp.dot(head_pair, down, preferred_element_type=F32)
    head_back = head_back[:logits] + head_back[logits:]
    for q in range(GROUP):
        side_src[q, images:, :] = head_back
    total = pair_out[p]
    for o in others:
        moves[3, o].wait_recv()
        total = total + parts_in[o - 1].astype(F32)
    xsum[...] = total
    swap = pltpu.make_async_remote_copy(
        src_ref=xsum, dst_ref=pair_in, send_sem=pair_send.at[0], recv_sem=pair_recv.at[0],
        device_id=(d, 1 - t), device_id_type=MESH,
    )
    swap.start()
    swap.wait()
    block_out = resid_ref[...].astype(F32) + (xsum[...] + pair_in[...])
    xhat, inv_std = normalize(block_out)
    xown[...] = xhat.astype(BF16)
    spread(4, lambda q: xown, xall.at[p])
    spread(5, lambda q: side_src.at[q], side_in.at[p])
    xall[p] = xown[...]
    side_in[p] = side_src[p]
    x_high, x_low = halves(xhat)
    nums = (((1,), (1,)), ((), ()))
    project = lax.dot_general(x_high, head_high, nums, preferred_element_type=F32)
    project += lax.dot_general(x_low, head_high, nums, preferred_element_type=F32)
    project += lax.dot_general(x_high, head_low, nums, preferred_element_type=F32)
    project_ref[...] = project * (1.0 / width)
    landed(4)
    back = jnp.dot(xall[...].reshape(rows, width), down, preferred_element_type=F32)
    back_src[...] = back.reshape(GROUP, images, cols)
    spread(6, lambda q: back_src.at[q], back_in.at[p])
    back_in[p] = back_src[p]
    landed(5)
    chosen = jnp.zeros((2 * (images + logits), units_ref.shape[1]), F32)
    for q in range(GROUP):
        both = jnp.concatenate(halves(side_in[q]), axis=0)
        chosen += jnp.dot(both, onehot[q], preferred_element_type=F32)
    chosen = chosen[: images + logits] + chosen[images + logits :]
    pick_ref[:images] = chosen[:images] * picked * inv_std
    pick_ref[images : images + logits] = chosen[images:]
    landed(6)
    chosen = jnp.zeros((2 * images, units_ref.shape[1]), F32)
    for q in range(GROUP):
        both = jnp.concatenate(halves(back_in[q]), axis=0)
        chosen += jnp.dot(both, onehot[q], preferred_element_type=F32)
    pick_ref[images + logits :] = chosen[:images] + chosen[images:]
    pick_out[...] = pick_ref[:, : 2 * panel]
    swap = pltpu.make_async_remote_copy(
        src_ref=pick_out, dst_ref=pick_in, send_sem=pair_send.at[1], recv_sem=pair_recv.at[1],
        device_id=(d, 1 - t), device_id_type=MESH,
    )
    swap.start()
    swap.wait()
    top_ref[...] = jnp.where(t == 0, pick_out[...], pick_in[...])
    for copy in sent:
        copy.wait_send()
    for w, buf in enumerate((wu, wd)):
        for s in range(planes):
            @pl.when((z >= s) & (z < last))
            def _():
                hop(buf, w, z - s, s, 1).wait_send()

            @pl.when((z + s <= last) & (z > 0))
            def _():
                hop(buf, w, z + s, s, -1).wait_send()


def fused_front(normed, residual_in, w_up, w_down, gain, head, inputs, units, members, panel):
    images, width = normed.shape
    depth, hidden_dev = w_up.shape
    logits = head.shape[0]
    rows_dev = units.shape[1]
    planes = members // GROUP
    cols = hidden_dev // GROUP
    side = images + logits
    total = side + images
    dma = pltpu.SemaphoreType.DMA
    vmem = pl.BlockSpec(memory_space=pltpu.VMEM)
    hbm = pl.BlockSpec(memory_space=pltpu.HBM)
    return pl.pallas_call(
        functools.partial(front_kernel, planes, panel),
        out_shape=(
            jax.ShapeDtypeStruct((total, rows_dev), F32),
            jax.ShapeDtypeStruct((total, 2 * panel), F32),
            jax.ShapeDtypeStruct((images, logits), F32),
        ),
        in_specs=[hbm] * 4 + [vmem] * 4,
        out_specs=(vmem,) * 3,
        scratch_shapes=[
            pltpu.VMEM((images, width), BF16),
            pltpu.VMEM((images, width), BF16),
            pltpu.VMEM((GROUP, images, width), BF16),
            pltpu.VMEM((planes, GROUP, depth, cols), BF16),
            pltpu.VMEM((planes, GROUP, depth, cols), BF16),
            pltpu.VMEM((GROUP, images, width), BF16),
            pltpu.VMEM((GROUP - 1, images, width), BF16),
            pltpu.VMEM((GROUP, images, width), F32),
            pltpu.VMEM((images, width), F32),
            pltpu.VMEM((images, width), BF16),
            pltpu.VMEM((GROUP, images, width), BF16),
            pltpu.VMEM((GROUP, side, cols), F32),
            pltpu.VMEM((GROUP, side, cols), F32),
            pltpu.VMEM((GROUP, images, cols), F32),
            pltpu.VMEM((GROUP, images, cols), F32),
            pltpu.VMEM((GROUP, cols, rows_dev), BF16),
            pltpu.VMEM((images, width), F32),
            pltpu.VMEM((total, 2 * panel), F32),
            pltpu.VMEM((total, 2 * panel), F32),
            dma((4,)),
            dma((7, GROUP)),
            dma((7, GROUP)),
            dma((2, planes)),
            dma((2, planes)),
            dma((2, planes)),
            dma((2, planes)),
            dma((2,)),
            dma((2,)),
        ],
        compiler_params=pltpu.CompilerParams(
            collective_id=0, has_side_effects=True, vmem_limit_bytes=48 * 1024 * 1024
        ),
        cost_estimate=pl.CostEstimate(
            flops=16 * images * width * hidden_dev,
            bytes_accessed=800 * depth * hidden_dev,
            transcendentals=2 * images * hidden_dev,
        ),
    )(normed, residual_in, w_up, w_down.T, gain, head, inputs, units)


def tail_kernel(
    panel, gain_ref, bent_ref, head_ref, top_gain_ref, top_bent_ref, top_head_ref, project_ref,
    panels_ref, corner_ref, inverses_ref, out_ref,
):
    t = lax.axis_index("tensor")
    images, rows_dev = gain_ref.shape
    logits = head_ref.shape[0]
    project = project_ref[...].reshape(images, logits, 1)

    def jacobian(gain, head, bent):
        value = gain[:, None, :] * (head[None, :, :] - project * bent[:, None, :])
        return value.reshape(images * logits, gain.shape[1]).astype(BF16)

    def solve(block, inverse):
        return lax.dot_general(
            block, inverse, (((1,), (1,)), ((), ())), preferred_element_type=F32
        ).astype(BF16)

    top = jacobian(top_gain_ref[...], top_head_ref[...], top_bent_ref[...])
    first = solve(top[:, :panel], inverses_ref[0])
    second_in = top[:, panel:].astype(F32) - jnp.dot(
        first, corner_ref[...], preferred_element_type=F32
    )
    second = solve(second_in.astype(BF16), inverses_ref[1])
    solved = jnp.concatenate([first, second], axis=1)
    lower = panels_ref[...].reshape(2 * panel, rows_dev)
    update = jnp.dot(solved, lower, preferred_element_type=F32)
    jac = jacobian(gain_ref[...], head_ref[...], bent_ref[...])
    below = jac.astype(F32) - update
    out_ref[:, 2 * panel :] = below[:, 2 * panel :].astype(BF16)
    out_ref[:, : 2 * panel] = jnp.where(
        t == 0, solved.astype(F32), below[:, : 2 * panel]
    ).astype(BF16)


def tail(pick, top, project, gathered, corner, inverses, images, logits):
    panel = inverses.shape[1]
    rows_dev = pick.shape[1]
    step = 16 if images % 16 == 0 else images

    def rows(count, columns):
        return pl.BlockSpec((count, columns), lambda i: (i, 0))

    def whole(*shape):
        return pl.BlockSpec(shape, lambda i: (0,) * len(shape))

    def cut(values):
        return values[:images], values[images + logits :], values[images : images + logits]

    return pl.pallas_call(
        functools.partial(tail_kernel, panel),
        grid=(images // step,),
        out_shape=jax.ShapeDtypeStruct((images * logits, rows_dev), BF16),
        in_specs=[
            rows(step, rows_dev), rows(step, rows_dev), whole(logits, rows_dev),
            rows(step, 2 * panel), rows(step, 2 * panel), whole(logits, 2 * panel),
            rows(step * logits, 1),
            whole(2, panel, rows_dev), whole(panel, panel), whole(2, panel, panel),
        ],
        out_specs=rows(step * logits, rows_dev),
        compiler_params=pltpu.CompilerParams(vmem_limit_bytes=40 * 1024 * 1024),
    )(
        *cut(pick), *cut(top), project.reshape(images * logits, 1), gathered, corner, inverses
    )


def plain_front(normed, residual_in, w_up, w_down, head_pair):
    images = normed.shape[0]
    logits = head_pair.shape[0] // 2
    up_pre = jnp.dot(
        normed, lax.all_gather(w_up, "dp", axis=0, tiled=True), preferred_element_type=F32
    )
    activ, slope = gelu_parts(up_pre)
    down_full = lax.all_gather(w_down, "dp", axis=1, tiled=True)
    partial_out = jnp.dot(activ.astype(BF16), down_full, preferred_element_type=F32)
    block_out = residual_in.astype(F32) + lax.psum(partial_out, "tensor")
    xhat, inv_std = normalize(block_out)
    both = jnp.concatenate([head_pair, xhat.astype(BF16)], axis=0)
    out = lax.dot_general(both, down_full, (((1,), (1,)), ((), ())), preferred_element_type=F32)
    head_back = out[:logits] + out[logits : 2 * logits]
    return jnp.concatenate([slope, head_back], axis=0), out[2 * logits :], xhat, inv_std


def from_first(value, ranks, tensor_rank):
    if ranks == 2:
        other = lax.ppermute(value, "tensor", [(0, 1)])
        return jnp.where(tensor_rank == 0, value, other)
    return lax.psum(jnp.where(tensor_rank == 0, value, jnp.zeros_like(value)), "tensor")


def body(
    members,
    ranks,
    normed,
    residual_in,
    w_up,
    w_down,
    final_gain,
    head_cols,
    sub_inputs,
    sub_hidden,
    panels,
    inverses,
):
    images, width = normed.shape
    hidden_dev = w_up.shape[1]
    logits = head_cols.shape[1]
    panel = inverses.shape[1]
    rows_dev = sub_inputs.shape[0]
    tensor_rank = lax.axis_index("tensor")

    gathered = lax.all_gather(panels, "dp", axis=1, tiled=True)
    corner = from_first(gathered[0, :, panel : 2 * panel], ranks, tensor_rank)
    local_hidden = sub_hidden - tensor_rank * hidden_dev

    fits = (
        ranks == 2
        and members % GROUP == 0
        and hidden_dev % (GROUP * 128) == 0
        and w_up.shape[0] % 16 == 0
        and images % 16 == 0
    )
    if fits:
        pick, top, project = fused_front(
            normed, residual_in, w_up, w_down, final_gain[None, :], head_cols.T,
            sub_inputs[None, :], local_hidden[None, :], members, panel,
        )
    else:
        scaled_head = (final_gain[:, None] * head_cols.astype(F32)).T
        centred_head = scaled_head - jnp.mean(scaled_head, axis=1, keepdims=True)
        head_pair = jnp.concatenate(halves(centred_head), axis=0)
        side, back, xhat, inv_std = plain_front(normed, residual_in, w_up, w_down, head_pair)
        project = lax.dot_general(
            xhat, centred_head, (((1,), (1,)), ((), ())), precision=lax.Precision.HIGHEST
        ) / width
        picked = jnp.take(normed, sub_inputs, axis=1).astype(F32)
        chosen = jnp.take(jnp.concatenate([side, back], axis=0), local_hidden, axis=1)
        pick = jnp.concatenate([chosen[:images] * picked * inv_std, chosen[images:]], axis=0)
        top = from_first(pick[:, : 2 * panel], ranks, tensor_rank)
    result = tail(pick, top, project, gathered, corner, inverses, images, logits)
    return result.reshape(images, logits, rows_dev)


def solution(mesh):
    in_specs = (
        P("dp", None),
        P("dp", None),
        P("dp", "tensor"),
        P("tensor", "dp"),
        P(),
        P(),
        P("tensor"),
        P("tensor"),
        P(None, "dp", "tensor"),
        P(),
    )
    out_specs = P("dp", None, "tensor")
    return jax.shard_map(
        functools.partial(body, mesh.shape["dp"], mesh.shape["tensor"]),
        mesh=mesh, in_specs=in_specs, out_specs=out_specs, check_vma=False,
    )
```

time: 200 us -> 147 us (0.73)
  local copies, waits for them, and re-layouts: 46.1 us -> 8.51 us
  Pallas kernels: 98.1 us -> 119 us
  waiting for transfers between devices: 19.6 us -> 1.66 us
  matrix products: 8.43 us -> 0 us
  other arithmetic: 8.33 us -> 1.61 us
  starting transfers between devices: 4.86 us -> 2.28 us
    pallas_call x1 -> x2, Pallas kernels: 98.1 us -> 119 us  [the longest x1 115 us: fused_front(): pl.pallas_call(functools.partial(front_kernel, planes, panel), out_shape=...]
    all_gather x1, waiting for transfers between devices: 19.5 us -> 0.02 us  [body(): gathered = lax.all_gather(panels, 'dp', axis=1, tiled=True)]
    mul x6 -> x0, local copies, waits for them, and re-layouts: 16 us -> none  [the longest x3 7.98 us: jacobian(): project[:, :, None] * bent[:, None, :]]
    dot_general x4 -> x0, matrix products: 8.43 us -> none  [the longest x1 6.23 us: body(): update = jnp.dot(solved, lower, preferred_element_type=F32)]
    sub x2 -> x0, local copies, waits for them, and re-layouts: 7.93 us -> none  [jacobian(): head_back[None, :, :] - project[:, :, None] * bent[:, None, :]]
    gather x2 -> x0, local copies, waits for them, and re-layouts: 7.88 us -> none  [the longest x1 4.68 us: body(): jnp.take(jnp.concatenate([side, back], axis=0), local_hidden, axis=1)]
    concatenate x2 -> x0, local copies, waits for them, and re-layouts: 4.52 us -> none  [the longest x1 2.56 us: body(): result = jnp.concatenate([head_part, below[:, 2 * panel:]], axis=1)]
    slice x11 -> x4, local copies, waits for them, and re-layouts: 3.52 us -> 0.08 us  [the longest x2 0.07 us: cut(): values[images + logits:]]
  transfers between devices with their start and end apart: 3 -> 2, of which waited for: 1 -> 1; matrix products, arithmetic and copies ran while one was open for 22% -> 1% of each run, Pallas kernels for 49% -> 78%
where the time goes in v2:
time: 147 us; the launch traced here: 146 us
  Pallas kernels  119 us (81%)
  between operations  13.5 us (9%)
  local copies, waits for them, and re-layouts  8.51 us (6%)
  starting transfers between devices  2.28 us (2%)
  waiting for transfers between devices  1.66 us (1%)
  other arithmetic  1.61 us (1%)
    pallas_call x1, Pallas kernels, fused_front(): pl.pallas_call(functools.partial(front_kernel, planes, panel), out_shape=...  115 us
    unnamed x16, local copies, waits for them, and re-layouts  6.52 us
    pallas_call x1, Pallas kernels, tail(): pl.pallas_call(functools.partial(tail_kernel, panel), grid=(images // ste...  4.09 us
  transfers between devices with their start and end apart: 2, of which 1 were waited for; matrix products, arithmetic and copies ran while one was open for 1% of the time, Pallas kernels for 78%

profile of v2, /device:TPU:0, one launch (start us, length us, event | category | flops | bytes accessed | tf_op | source)
XLA Modules:
  0.0 146.3 jit_solution(10974547632857989049)
XLA Ops:
  6.5 0.0 all-gather.2.cloned.1.call-start
  6.5 0.7 all-gather.2.cloned.1.call-update
  7.3 0.7 broadcast_in_dim.9.gain_ref
  8.0 0.7 broadcast_subtract_fusion
  8.7 0.0 copy-start.2
  8.7 1.0 copy-done.2
  9.7 0.0 copy-start.3
  9.7 1.0 copy-done.3
  10.7 0.0 copy-start.4
  10.7 0.9 copy-done.4
  11.6 0.0 copy-start.5
  11.6 0.9 copy-done.5
  12.5 0.0 copy-start.6
  12.5 0.8 copy-done.6
  13.3 0.0 copy-start.7
  13.3 0.7 copy-done.7
  14.0 114.7 %shard_map.100 = (f32[144,1024]{1,0:T(8,128)S(1)}, f32[144,512]{1,0:T(8,128)S(1)}, f32[64,16]{1,0:T(8,128)S(1)}) custom-call(bf16[64,1280]{1,0:T(8,128)(2,1)S(1)} %copy-done.4, bf16[64,1280]{1,0:T(8,128)(2,1)S(1)} %copy-done.5, bf16[80,2560]{1,0:T(8,128)(2,1)S(1)} %copy-done.2, bf16[80,2560]{1,0:T(8,128)(2,1)S(1)} %bitcast.10, ...), custom_call_target="tpu_custom_call" | custom-call | flops 3355443200 | bytes 163840000 | tf_op jit(solution)/shard_map/pallas_call | solution.py:256
  128.6 0.0 copy-start.1
  128.7 0.3 reshape.8.project_ref
  129.0 0.0 all-gather.2.cloned.1.call-done.panels_ref
  129.1 0.9 slice_bitcast_fusion
  130.0 2.3 %collective-permute-start = (bf16[256,256]{1,0:T(8,128)(2,1)S(1)}, bf16[256,256]{1,0:T(8,128)(2,1)S(1)}, u32[]{:S(2)}, u32[]{:S(2)}) collective-permute-start(bf16[256,256]{1,0:T(8,128)(2,1)S(1)} %slice_bitcast_fusion), channel_id=1, source_target_pairs={{0,1},{2,3},{4,5},{6,7},{8,9},{10,11},{12,13},{14,15},{16,17},{18,... | collective-permute-start | bytes 393224 | tf_op jit(solution)/shard_map/ppermute | solution.py:391
  132.3 0.9 collective-permute-done
  133.2 0.9 broadcast_select_fusion.corner_ref
  134.2 0.0 copy-done.1
  134.2 0.0 copy-start
  134.2 1.2 copy-done
  135.4 4.1 %shard_map.101 = bf16[1024,1024]{1,0:T(8,128)(2,1)} custom-call(f32[64,1024]{1,0:T(8,128)S(1)} %get-tuple-element.12.gain_ref, f32[64,1024]{1,0:T(8,128)S(1)} %get-tuple-element.11.bent_ref, f32[16,1024]{1,0:T(8,128)S(1)} %slice.23.head_ref, f32[64,512]{1,0:T(8,128)S(1)} %get-tuple-element.14.top_gain_ref, f32[64,512]{1,0:T(8,128)S(1)} %get-tuple-element.13.top_bent_ref, ...), custom_call_target="tpu_custom_call" | custom-call | tf_op jit(solution)/shard_map/pallas_call | solution.py:355
  (4 shorter events, 0.1 us)
Async XLA Ops:
  6.5 122.5 %all-gather.2.cloned.1.call-start = ((), (), s32[]{:S(2)}) async-start(), calls=%async_computation | async-start | bytes 1114112 | tf_op jit(solution)/shard_map/all_gather | solution.py:417
  8.7 1.0 copy-start.2
  9.7 1.0 copy-start.3
  10.7 0.9 copy-start.4
  11.6 0.9 copy-start.5
  12.5 0.8 copy-start.6
  13.3 0.7 copy-start.7
  128.6 5.5 %copy-start.1 = (bf16[2,256,256]{2,1,0:T(8,128)(2,1)S(1)}, bf16[2,256,256]{2,1,0:T(8,128)(2,1)}, u32[]{:S(2)}) copy-start(bf16[2,256,256]{2,1,0:T(8,128)(2,1)} %inverses_ref.1) | copy-start | bytes 786436
  130.0 3.3 %collective-permute-start = (bf16[256,256]{1,0:T(8,128)(2,1)S(1)}, bf16[256,256]{1,0:T(8,128)(2,1)S(1)}, u32[]{:S(2)}, u32[]{:S(2)}) collective-permute-start(bf16[256,256]{1,0:T(8,128)(2,1)S(1)} %slice_bitcast_fusion), channel_id=1, source_target_pairs={{0,1},{2,3},{4,5},{6,7},{8,9},{10,11},{12,13},{14,15},{16,17},{18,... | collective-permute-start | bytes 393224 | tf_op jit(solution)/shard_map/ppermute | solution.py:391
  134.2 1.2 copy-start
Sparse Core Ops, SparseCore 0:
  10.1 59.3 all-gather.1

commit v3 on v2

--- a/solution.py
+++ b/solution.py
@@ -40,10 +40,11 @@
 def front_kernel(
     planes,
     panel,
-    normed_hbm, resid_hbm, wup_ref, wdt_ref, gain_ref, head_ref, inputs_ref, units_ref,
-    pick_ref, top_ref, project_ref,
+    normed_hbm, resid_hbm, wup_ref, wdt_ref, gain_ref, head_ref, inputs_ref, units_ref, panels_hbm,
+    pick_ref, top_ref, project_ref, panels_ref, corner_ref,
     normed_ref, resid_ref, nall, wu, wd, part, parts_in, pair_out, pair_in, xown, xall,
-    side_src, side_in, back_src, back_in, onehot, xsum, pick_out, pick_in,
+    slope_src, slope_in, head_src, head_in, back_src, back_in, onehot, xsum, pick_out, pick_in,
+    pan, corner_out, corner_in,
     local_sem, flat_send, flat_recv, up_send, up_recv, dn_send, dn_recv, pair_send, pair_recv,
 ):
     d = lax.axis_index("dp")
@@ -86,6 +87,7 @@
         pltpu.make_async_copy(block(wdt_ref, p), wd.at[z, p], local_sem.at[1]),
         pltpu.make_async_copy(normed_hbm, normed_ref, local_sem.at[2]),
         pltpu.make_async_copy(resid_hbm, resid_ref, local_sem.at[3]),
+        pltpu.make_async_copy(panels_hbm, pan.at[z, p], local_sem.at[4]),
     ]
     moves = {}
 
@@ -111,6 +113,14 @@
     head_high, head_low = halves(head)
     head_pair = jnp.concatenate([head_high, head_low], axis=0)
 
+    def selected(parts):
+        chosen = 0.0
+        for q in range(GROUP):
+            both = jnp.concatenate(halves(parts[q]), axis=0)
+            chosen += jnp.dot(both, onehot[q], preferred_element_type=F32)
+        count = parts.shape[1]
+        return chosen[:count] + chosen[count:]
+
     def hop(buf, w, src, s, step):
         send, recv = (up_send, up_recv) if step > 0 else (dn_send, dn_recv)
         return pltpu.make_async_remote_copy(
@@ -145,6 +155,8 @@
     landed(1)
     relay(wd, 1, 0)
     spread(2, lambda q: normed_ref, nall.at[p])
+    spread(7, lambda q: panels_hbm, pan.at[z, p])
+    own[4].wait()
     picked = pick_columns(normed_ref[...], inputs_ref[...], width)
     chunk = lax.broadcasted_iota(jnp.int32, (cols, units_ref.shape[1]), 0)
     relay(wu, 0, 1)
@@ -153,6 +165,8 @@
     landed(2)
     for s in range(2, planes):
         relay(wu, 0, s)
+        if s == 2:
+            relay(wd, 1, 1)
 
     rows = GROUP * images
     up_pre = jnp.dot(
@@ -160,10 +174,16 @@
     )
     activ, slope = gelu_parts(up_pre)
     hidden = activ.astype(BF16)
-    side_src[:, :images, :] = slope.reshape(GROUP, images, cols)
-
-    for s in range(1, planes):
+    slope_src[...] = slope.reshape(GROUP, images, cols)
+    spread(5, lambda q: slope_src.at[q], slope_in.at[p])
+    slope_in[p] = slope_src[p]
+    for s in range(2, planes - 1):
         relay(wd, 1, s)
+    landed(5)
+    pick_ref[:images] = selected(slope_in) * picked
+    landed(7)
+    relay(wd, 1, planes - 1)
+    relay(pan, 2, 0)
     down = wd[...].reshape(width, cols)
     partial = lax.dot_general(hidden, down, (((1,), (1,)), ((), ())), preferred_element_type=F32)
     pair_out[...] = partial.reshape(GROUP, images, width)
@@ -175,8 +195,9 @@
         sent.append(copy)
     head_back = jnp.dot(head_pair, down, preferred_element_type=F32)
     head_back = head_back[:logits] + head_back[logits:]
-    for q in range(GROUP):
-        side_src[q, images:, :] = head_back
+    head_src[...] = head_back
+    spread(8, lambda q: head_src, head_in.at[p])
+    head_in[p] = head_back
     total = pair_out[p]
     for o in others:
         moves[3, o].wait_recv()
@@ -192,9 +213,8 @@
     xhat, inv_std = normalize(block_out)
     xown[...] = xhat.astype(BF16)
     spread(4, lambda q: xown, xall.at[p])
-    spread(5, lambda q: side_src.at[q], side_in.at[p])
+    relay(pan, 2, 1)
     xall[p] = xown[...]
-    side_in[p] = side_src[p]
     x_high, x_low = halves(xhat)
     nums = (((1,), (1,)), ((), ()))
     project = lax.dot_general(x_high, head_high, nums, preferred_element_type=F32)
@@ -203,34 +223,43 @@
     project_ref[...] = project * (1.0 / width)
     landed(4)
     back = jnp.dot(xall[...].reshape(rows, width), down, preferred_element_type=F32)
-    back_src[...] = back.reshape(GROUP, images, cols)
+    back_src[...] = back.astype(BF16).reshape(GROUP, images, cols)
     spread(6, lambda q: back_src.at[q], back_in.at[p])
     back_in[p] = back_src[p]
-    landed(5)
-    chosen = jnp.zeros((2 * (images + logits), units_ref.shape[1]), F32)
+    landed(8)
+    pick_ref[:images] = pick_ref[:images] * inv_std
+    pick_ref[images : images + logits] = selected(head_in)
+    for s in range(2, planes):
+        relay(pan, 2, s)
+    for q in range(2):
+        panels_ref[q] = pan[:, :, q].reshape(panels_ref.shape[1:])
+    corner_out[...] = panels_ref[0, :, panel : 2 * panel]
+
+    def swap(src, dst, i):
+        return pltpu.make_async_remote_copy(
+            src_ref=src, dst_ref=dst, send_sem=pair_send.at[i], recv_sem=pair_recv.at[i],
+            device_id=(d, 1 - t), device_id_type=MESH,
+        )
+
+    corner_swap = swap(corner_out, corner_in, 2)
+    corner_swap.start()
+    landed(6)
+    chosen = jnp.zeros((images, units_ref.shape[1]), F32)
     for q in range(GROUP):
-        both = jnp.concatenate(halves(side_in[q]), axis=0)
-        chosen += jnp.dot(both, onehot[q], preferred_element_type=F32)
-    chosen = chosen[: images + logits] + chosen[images + logits :]
-    pick_ref[:images] = chosen[:images] * picked * inv_std
-    pick_ref[images : images + logits] = chosen[images:]
-    landed(6)
-    chosen = jnp.zeros((2 * images, units_ref.shape[1]), F32)
-    for q in range(GROUP):
-        both = jnp.concatenate(halves(back_in[q]), axis=0)
-        chosen += jnp.dot(both, onehot[q], preferred_element_type=F32)
-    pick_ref[images + logits :] = chosen[:images] + chosen[images:]
+        chosen += jnp.dot(back_in[q], onehot[q], preferred_element_type=F32)
+    pick_ref[images + logits :] = chosen
     pick_out[...] = pick_ref[:, : 2 * panel]
-    swap = pltpu.make_async_remote_copy(
-        src_ref=pick_out, dst_ref=pick_in, send_sem=pair_send.at[1], recv_sem=pair_recv.at[1],
-        device_id=(d, 1 - t), device_id_type=MESH,
-    )
-    swap.start()
-    swap.wait()
+    pick_swap = swap(pick_out, pick_in, 1)
+    pick_swap.start()
+    corner_swap.wait()
+    pick_swap.wait()
     top_ref[...] = jnp.where(t == 0, pick_out[...], pick_in[...])
+    corner_ref[...] = jnp.where(
+        t == 0, corner_out[...].astype(F32), corner_in[...].astype(F32)
+    ).astype(BF16)
     for copy in sent:
         copy.wait_send()
-    for w, buf in enumerate((wu, wd)):
+    for w, buf in enumerate((wu, wd, pan)):
         for s in range(planes):
             @pl.when((z >= s) & (z < last))
             def _():
@@ -241,10 +270,11 @@
                 hop(buf, w, z + s, s, -1).wait_send()
 
 
-def fused_front(normed, residual_in, w_up, w_down, gain, head, inputs, units, members, panel):
+def fused_front(normed, residual_in, w_up, w_down, gain, head, inputs, units, panels, members):
     images, width = normed.shape
     depth, hidden_dev = w_up.shape
     logits = head.shape[0]
+    panel = panels.shape[1] * members
     rows_dev = units.shape[1]
     planes = members // GROUP
     cols = hidden_dev // GROUP
@@ -259,9 +289,11 @@
             jax.ShapeDtypeStruct((total, rows_dev), F32),
             jax.ShapeDtypeStruct((total, 2 * panel), F32),
             jax.ShapeDtypeStruct((images, logits), F32),
+            jax.ShapeDtypeStruct((2, panel, rows_dev), BF16),
+            jax.ShapeDtypeStruct((panel, panel), BF16),
         ),
-        in_specs=[hbm] * 4 + [vmem] * 4,
-        out_specs=(vmem,) * 3,
+        in_specs=[hbm] * 4 + [vmem] * 4 + [hbm],
+        out_specs=(vmem,) * 5,
         scratch_shapes=[
             pltpu.VMEM((images, width), BF16),
             pltpu.VMEM((images, width), BF16),
@@ -274,23 +306,28 @@
             pltpu.VMEM((images, width), F32),
             pltpu.VMEM((images, width), BF16),
             pltpu.VMEM((GROUP, images, width), BF16),
-            pltpu.VMEM((GROUP, side, cols), F32),
-            pltpu.VMEM((GROUP, side, cols), F32),
             pltpu.VMEM((GROUP, images, cols), F32),
             pltpu.VMEM((GROUP, images, cols), F32),
+            pltpu.VMEM((logits, cols), F32),
+            pltpu.VMEM((GROUP, logits, cols), F32),
+            pltpu.VMEM((GROUP, images, cols), BF16),
+            pltpu.VMEM((GROUP, images, cols), BF16),
             pltpu.VMEM((GROUP, cols, rows_dev), BF16),
             pltpu.VMEM((images, width), F32),
             pltpu.VMEM((total, 2 * panel), F32),
             pltpu.VMEM((total, 2 * panel), F32),
-            dma((4,)),
-            dma((7, GROUP)),
-            dma((7, GROUP)),
-            dma((2, planes)),
-            dma((2, planes)),
-            dma((2, planes)),
-            dma((2, planes)),
-            dma((2,)),
-            dma((2,)),
+            pltpu.VMEM((planes, GROUP) + panels.shape, BF16),
+            pltpu.VMEM((panel, panel), BF16),
+            pltpu.VMEM((panel, panel), BF16),
+            dma((5,)),
+            dma((9, GROUP)),
+            dma((9, GROUP)),
+            dma((3, planes)),
+            dma((3, planes)),
+            dma((3, planes)),
+            dma((3, planes)),
+            dma((3,)),
+            dma((3,)),
         ],
         compiler_params=pltpu.CompilerParams(
             collective_id=0, has_side_effects=True, vmem_limit_bytes=48 * 1024 * 1024
@@ -300,7 +337,7 @@
             bytes_accessed=800 * depth * hidden_dev,
             transcendentals=2 * images * hidden_dev,
         ),
-    )(normed, residual_in, w_up, w_down.T, gain, head, inputs, units)
+    )(normed, residual_in, w_up, w_down.T, gain, head, inputs, units, panels)
 
 
 def tail_kernel(
@@ -386,10 +423,7 @@
     return jnp.concatenate([slope, head_back], axis=0), out[2 * logits :], xhat, inv_std
 
 
-def from_first(value, ranks, tensor_rank):
-    if ranks == 2:
-        other = lax.ppermute(value, "tensor", [(0, 1)])
-        return jnp.where(tensor_rank == 0, value, other)
+def from_first(value, tensor_rank):
     return lax.psum(jnp.where(tensor_rank == 0, value, jnp.zeros_like(value)), "tensor")
 
 
@@ -414,8 +448,6 @@
     rows_dev = sub_inputs.shape[0]
     tensor_rank = lax.axis_index("tensor")
 
-    gathered = lax.all_gather(panels, "dp", axis=1, tiled=True)
-    corner = from_first(gathered[0, :, panel : 2 * panel], ranks, tensor_rank)
     local_hidden = sub_hidden - tensor_rank * hidden_dev
 
     fits = (
@@ -424,13 +456,17 @@
         and hidden_dev % (GROUP * 128) == 0
         and w_up.shape[0] % 16 == 0
         and images % 16 == 0
+        and panels.shape[1] % 16 == 0
+        and members >= 3 * GROUP
     )
     if fits:
-        pick, top, project = fused_front(
+        pick, top, project, gathered, corner = fused_front(
             normed, residual_in, w_up, w_down, final_gain[None, :], head_cols.T,
-            sub_inputs[None, :], local_hidden[None, :], members, panel,
+            sub_inputs[None, :], local_hidden[None, :], panels, members,
         )
     else:
+        gathered = lax.all_gather(panels, "dp", axis=1, tiled=True)
+        corner = from_first(gathered[0, :, panel : 2 * panel], tensor_rank)
         scaled_head = (final_gain[:, None] * head_cols.astype(F32)).T
         centred_head = scaled_head - jnp.mean(scaled_head, axis=1, keepdims=True)
         head_pair = jnp.concatenate(halves(centred_head), axis=0)
@@ -441,7 +477,7 @@
         picked = jnp.take(normed, sub_inputs, axis=1).astype(F32)
         chosen = jnp.take(jnp.concatenate([side, back], axis=0), local_hidden, axis=1)
         pick = jnp.concatenate([chosen[:images] * picked * inv_std, chosen[images:]], axis=0)
-        top = from_first(pick[:, : 2 * panel], ranks, tensor_rank)
+        top = from_first(pick[:, : 2 * panel], tensor_rank)
     result = tail(pick, top, project, gathered, corner, inverses, images, logits)
     return result.reshape(images, logits, rows_dev)
 

time: 147 us -> 109 us (0.74)
  Pallas kernels: 119 us -> 99.8 us
  between operations: 13.5 us -> 0.07 us
  starting transfers between devices: 2.28 us -> 0 us
  waiting for transfers between devices: 1.66 us -> 0 us
    pallas_call x1, Pallas kernels: 115 us -> 95.7 us  [fused_front(): pl.pallas_call(functools.partial(front_kernel, planes, panel), out_shape=...]
    ppermute x1 -> x0, starting transfers between devices: 2.28 us -> none  [from_first(): other = lax.ppermute(value, 'tensor', [(0, 1)])]
  transfers between devices with their start and end apart: 2 -> 0, of which waited for: 1 -> 0; matrix products, arithmetic and copies ran while one was open for 1% -> 0% of each run, Pallas kernels for 78% -> 0%
where the time goes in v3:
time: 109 us; the launch traced here: 108 us
  Pallas kernels  99.8 us (92%)
  local copies, waits for them, and re-layouts  7.74 us (7%)
    pallas_call x1, Pallas kernels, fused_front(): pl.pallas_call(functools.partial(front_kernel, planes, panel), out_shape=...  95.7 us
    unnamed x16, local copies, waits for them, and re-layouts  6.68 us
    pallas_call x1, Pallas kernels, tail(): pl.pallas_call(functools.partial(tail_kernel, panel), grid=(images // ste...  4.09 us

profile of v3, /device:TPU:0, one launch (start us, length us, event | category | flops | bytes accessed | tf_op | source)
XLA Modules:
  0.0 108.2 jit_solution(3774354858793694832)
XLA Ops:
  0.0 0.7 broadcast_subtract_fusion
  0.7 0.7 broadcast_in_dim.9.gain_ref
  1.4 0.0 copy-start.1
  1.4 1.0 copy-done.1
  2.4 0.0 copy-start.2
  2.4 1.0 copy-done.2
  3.4 0.0 copy-start.3
  3.4 0.9 copy-done.3
  4.3 0.0 copy-start.4
  4.3 0.9 copy-done.4
  5.2 0.0 copy-start.5
  5.2 0.8 copy-done.5
  6.1 0.0 copy-start.6
  6.1 0.8 copy-done.6
  6.8 0.0 copy-start.7
  6.8 0.7 copy-done.7
  7.5 95.7 %shard_map.100 = (f32[144,1024]{1,0:T(8,128)S(1)}, f32[144,512]{1,0:T(8,128)S(1)}, f32[64,16]{1,0:T(8,128)S(1)}, bf16[2,256,1024]{2,1,0:T(8,128)(2,1)S(1)}, bf16[256,256]{1,0:T(8,128)(2,1)S(1)}) custom-call(bf16[64,1280]{1,0:T(8,128)(2,1)S(1)} %copy-done.3, bf16[64,1280]{1,0:T(8,128)(2,1)S(1)} %copy-done.4, bf16[80,2560]{1,0:T(8,128)(2,1)S(1)} %copy-done.1, ...), custom_call_target="tpu_custom_call" | custom-call | flops 3355443200 | bytes 163840000 | tf_op jit(solution)/shard_map/pallas_call | solution.py:286
  103.2 0.0 copy-start
  103.3 0.3 reshape.8.project_ref
  103.6 0.5 copy-done
  104.2 4.1 %shard_map.101 = bf16[1024,1024]{1,0:T(8,128)(2,1)} custom-call(f32[64,1024]{1,0:T(8,128)S(1)} %get-tuple-element.16.gain_ref, f32[64,1024]{1,0:T(8,128)S(1)} %get-tuple-element.15.bent_ref, f32[16,1024]{1,0:T(8,128)S(1)} %slice.20.head_ref, f32[64,512]{1,0:T(8,128)S(1)} %get-tuple-element.18.top_gain_ref, f32[64,512]{1,0:T(8,128)S(1)} %get-tuple-element.17.top_bent_ref, ...), custom_call_target="tpu_custom_call" | custom-call | tf_op jit(solution)/shard_map/pallas_call | solution.py:392
  (4 shorter events, 0.1 us)
Async XLA Ops:
  1.4 1.0 copy-start.1
  2.4 1.0 copy-start.2
  3.4 0.9 copy-start.3
  4.3 0.9 copy-start.4
  5.2 0.8 copy-start.5
  6.1 0.8 copy-start.6
  6.8 0.7 copy-start.7
  103.2 1.0 copy-start

commit v4 on v3

--- a/solution.py
+++ b/solution.py
@@ -105,6 +105,66 @@
     spread(0, lambda q: block(wup_ref, q), wu.at[z, p])
     for copy in own:
         copy.start()
+    def selected(parts):
+        chosen = 0.0
+        for q in range(GROUP):
+            both = jnp.concatenate(halves(parts[q]), axis=0)
+            chosen += jnp.dot(both, onehot[q], preferred_element_type=F32)
+        count = parts.shape[1]
+        return chosen[:count] + chosen[count:]
+
+    def hop(buf, w, src, s, step):
+        send, recv = (up_send, up_recv) if step > 0 else (dn_send, dn_recv)
+        return pltpu.make_async_remote_copy(
+            src_ref=buf.at[src], dst_ref=buf.at[src], send_sem=send.at[w, s], recv_sem=recv.at[w, s],
+            device_id=(d + step * GROUP, t), device_id_type=MESH,
+        )
+
+    def chunk_out(buf, w, q):
+        def send(step, sems, marks):
+            pltpu.make_async_remote_copy(
+                src_ref=buf.at[z, q], dst_ref=buf.at[z, q], send_sem=sems.at[w, 0],
+                recv_sem=marks.at[w, 0], device_id=(d + step * GROUP, t), device_id_type=MESH,
+            ).start()
+
+        @pl.when(z < last)
+        def _():
+            send(1, up_send, up_recv)
+
+        @pl.when(z > 0)
+        def _():
+            send(-1, dn_send, dn_recv)
+
+    def relay(buf, w, s):
+        @pl.when(z >= s)
+        def _():
+            if s > 0:
+                hop(buf, w, z - s, s - 1, 1).wait_recv()
+
+            @pl.when(z < last)
+            def _():
+                hop(buf, w, z - s, s, 1).start()
+
+        @pl.when(z + s <= last)
+        def _():
+            if s > 0:
+                hop(buf, w, z + s, s - 1, -1).wait_recv()
+
+            @pl.when(z > 0)
+            def _():
+                hop(buf, w, z + s, s, -1).start()
+
+    own[0].wait()
+    chunk_out(wu, 0, p)
+    for o in others:
+        moves[0, o].wait_recv()
+        chunk_out(wu, 0, p ^ o)
+    spread(1, lambda q: block(wdt_ref, q), wd.at[z, p])
+    own[1].wait()
+    chunk_out(wd, 1, p)
+    for o in others:
+        moves[1, o].wait_recv()
+        chunk_out(wd, 1, p ^ o)
     own[2].wait()
     own[3].wait()
     nall[p] = normed_ref[...]
@@ -112,48 +172,6 @@
     head = head - jnp.mean(head, axis=1, keepdims=True)
     head_high, head_low = halves(head)
     head_pair = jnp.concatenate([head_high, head_low], axis=0)
-
-    def selected(parts):
-        chosen = 0.0
-        for q in range(GROUP):
-            both = jnp.concatenate(halves(parts[q]), axis=0)
-            chosen += jnp.dot(both, onehot[q], preferred_element_type=F32)
-        count = parts.shape[1]
-        return chosen[:count] + chosen[count:]
-
-    def hop(buf, w, src, s, step):
-        send, recv = (up_send, up_recv) if step > 0 else (dn_send, dn_recv)
-        return pltpu.make_async_remote_copy(
-            src_ref=buf.at[src], dst_ref=buf.at[src], send_sem=send.at[w, s], recv_sem=recv.at[w, s],
-            device_id=(d + step * GROUP, t), device_id_type=MESH,
-        )
-
-    def relay(buf, w, s):
-        @pl.when(z >= s)
-        def _():
-            if s > 0:
-                hop(buf, w, z - s, s - 1, 1).wait_recv()
-
-            @pl.when(z < last)
-            def _():
-                hop(buf, w, z - s, s, 1).start()
-
-        @pl.when(z + s <= last)
-        def _():
-            if s > 0:
-                hop(buf, w, z + s, s - 1, -1).wait_recv()
-
-            @pl.when(z > 0)
-            def _():
-                hop(buf, w, z + s, s, -1).start()
-
-    own[0].wait()
-    landed(0)
-    relay(wu, 0, 0)
-    spread(1, lambda q: block(wdt_ref, q), wd.at[z, p])
-    own[1].wait()
-    landed(1)
-    relay(wd, 1, 0)
     spread(2, lambda q: normed_ref, nall.at[p])
     spread(7, lambda q: panels_hbm, pan.at[z, p])
     own[4].wait()
@@ -330,7 +348,7 @@
             dma((3,)),
         ],
         compiler_params=pltpu.CompilerParams(
-            collective_id=0, has_side_effects=True, vmem_limit_bytes=48 * 1024 * 1024
+            collective_id=0, has_side_effects=True, vmem_limit_bytes=60 * 1024 * 1024
         ),
         cost_estimate=pl.CostEstimate(
             flops=16 * images * width * hidden_dev,

time: 109 us -> 105 us (0.963)
  Pallas kernels: 99.8 us -> 97.6 us
  local copies, waits for them, and re-layouts: 7.74 us -> 6.12 us
    unnamed x16 -> x6, local copies, waits for them, and re-layouts: 6.68 us -> 0.01 us
    pallas_call x1, Pallas kernels: 95.7 us -> 93.5 us  [fused_front(): pl.pallas_call(functools.partial(front_kernel, planes, panel), out_shape=...]
    slice x2, local copies, waits for them, and re-layouts: 0.06 us -> 2.05 us  [cut(): values[images + logits:]]
    slice x2, local copies, waits for them, and re-layouts: 0.01 us -> 1.71 us  [cut(): values[images:images + logits]]
where the time goes in v4:
time: 105 us
  Pallas kernels  97.6 us (93%)
  local copies, waits for them, and re-layouts  6.12 us (6%)
  other arithmetic  1.28 us (1%)
    pallas_call x1, Pallas kernels, fused_front(): pl.pallas_call(functools.partial(front_kernel, planes, panel), out_shape=...  93.5 us
    pallas_call x1, Pallas kernels, tail(): pl.pallas_call(functools.partial(tail_kernel, panel), grid=(images // ste...  4.12 us

profile of v4, /device:TPU:0, one launch (start us, length us, event | category | flops | bytes accessed | tf_op | source)
XLA Modules:
  0.0 105.1 jit_solution(8384444390295235331)
XLA Ops:
  0.0 1.3 %broadcast_subtract_fusion = s32[1024]{0:T(1024)} fusion(s32[1024]{0:T(1024)} %param.17, s32[]{:T(128)S(6)} %mul.3), kind=kLoop, calls=%fused_computation | loop fusion | flops 1024 | bytes 8196 | tf_op jit(solution)/shard_map/sub | solution.py:469
  1.3 1.3 %broadcast_in_dim.9.gain_ref = f32[1,1280]{1,0:T(1,128)} reshape(f32[1280]{0:T(1024)} %param.14) | data formatting | bytes 10240 | tf_op jit(solution)/shard_map/broadcast_in_dim | solution.py:482
  2.6 93.5 %shard_map.100 = (f32[144,1024]{1,0:T(8,128)}, f32[144,512]{1,0:T(8,128)}, f32[64,16]{1,0:T(8,128)}, bf16[2,256,1024]{2,1,0:T(8,128)(2,1)}, bf16[256,256]{1,0:T(8,128)(2,1)}) custom-call(bf16[64,1280]{1,0:T(8,128)(2,1)} %normed_hbm.1, bf16[64,1280]{1,0:T(8,128)(2,1)} %resid_hbm.1, bf16[80,2560]{1,0:T(8,128)(2,1)} %wup_ref.1, bf16[80,2560]{1,0:T(8,128)(2,1)} %bitcast.6, ...), custom_call_target="tpu_custom_call" | custom-call | flops 3355443200 | bytes 163840000 | tf_op jit(solution)/shard_map/pallas_call | solution.py:304
  96.0 0.0 copy-start
  96.1 0.0 copy-start.1
  96.1 0.0 copy-start.2
  96.1 0.9 slice.23.top_head_ref
  96.9 1.0 fusion.1
  97.9 0.8 slice.20.head_ref
  98.8 1.1 %fusion = (f32[64,1024]{1,0:T(8,128)S(1)}, f32[64,1024]{1,0:T(8,128)S(1)}) fusion(f32[144,1024]{1,0:T(8,128)} %get-tuple-element.10), kind=kLoop, calls=%fused_computation.1 | loop fusion | bytes 1048576 | tf_op jit(solution)/shard_map/slice | solution.py:408
  99.8 1.0 reshape.8.project_ref
  100.9 0.0 copy-done
  100.9 0.0 copy-done.1
  100.9 0.0 copy-done.2
  100.9 4.1 %shard_map.101 = bf16[1024,1024]{1,0:T(8,128)(2,1)} custom-call(f32[64,1024]{1,0:T(8,128)S(1)} %get-tuple-element.16.gain_ref, f32[64,1024]{1,0:T(8,128)S(1)} %get-tuple-element.15.bent_ref, f32[16,1024]{1,0:T(8,128)S(1)} %slice.20.head_ref, f32[64,512]{1,0:T(8,128)S(1)} %get-tuple-element.18.top_gain_ref, f32[64,512]{1,0:T(8,128)S(1)} %get-tuple-element.17.top_bent_ref, ...), custom_call_target="tpu_custom_call" | custom-call | tf_op jit(solution)/shard_map/pallas_call | solution.py:410
Async XLA Ops:
  96.0 4.9 %copy-start = (bf16[2,256,1024]{2,1,0:T(8,128)(2,1)S(1)}, bf16[2,256,1024]{2,1,0:T(8,128)(2,1)}, u32[]{:S(2)}) copy-start(bf16[2,256,1024]{2,1,0:T(8,128)(2,1)} %get-tuple-element.13.panels_ref) | copy-start | bytes 3145732
  96.1 4.9 %copy-start.1 = (bf16[2,256,256]{2,1,0:T(8,128)(2,1)S(1)}, bf16[2,256,256]{2,1,0:T(8,128)(2,1)}, u32[]{:S(2)}) copy-start(bf16[2,256,256]{2,1,0:T(8,128)(2,1)} %inverses_ref.1) | copy-start | bytes 786436
  96.1 4.9 %copy-start.2 = (bf16[256,256]{1,0:T(8,128)(2,1)S(1)}, bf16[256,256]{1,0:T(8,128)(2,1)}, u32[]{:S(2)}) copy-start(bf16[256,256]{1,0:T(8,128)(2,1)} %get-tuple-element.14.corner_ref) | copy-start | bytes 393220

commit v5 on v4

--- a/solution.py
+++ b/solution.py
@@ -179,7 +179,7 @@
     chunk = lax.broadcasted_iota(jnp.int32, (cols, units_ref.shape[1]), 0)
     relay(wu, 0, 1)
     for q in range(GROUP):
-        onehot[q] = jnp.where(chunk + q * cols == units_ref[...], 1.0, 0.0).astype(BF16)
+        onehot[q] = jnp.where(chunk + (t * GROUP + q) * cols == units_ref[...], 1.0, 0.0).astype(BF16)
     landed(2)
     for s in range(2, planes):
         relay(wu, 0, s)
@@ -396,7 +396,8 @@
 def tail(pick, top, project, gathered, corner, inverses, images, logits):
     panel = inverses.shape[1]
     rows_dev = pick.shape[1]
-    step = 16 if images % 16 == 0 else images
+    step = logits
+    last = images // step
 
     def rows(count, columns):
         return pl.BlockSpec((count, columns), lambda i: (i, 0))
@@ -404,23 +405,27 @@
     def whole(*shape):
         return pl.BlockSpec(shape, lambda i: (0,) * len(shape))
 
-    def cut(values):
-        return values[:images], values[images + logits :], values[images : images + logits]
+    def parts(columns):
+        return [
+            pl.BlockSpec((step, columns), lambda i: (i, 0)),
+            pl.BlockSpec((step, columns), lambda i: (last + 1 + i, 0)),
+            pl.BlockSpec((step, columns), lambda i: (last, 0)),
+        ]
 
     return pl.pallas_call(
         functools.partial(tail_kernel, panel),
         grid=(images // step,),
         out_shape=jax.ShapeDtypeStruct((images * logits, rows_dev), BF16),
         in_specs=[
-            rows(step, rows_dev), rows(step, rows_dev), whole(logits, rows_dev),
-            rows(step, 2 * panel), rows(step, 2 * panel), whole(logits, 2 * panel),
+            *parts(rows_dev),
+            *parts(2 * panel),
             rows(step * logits, 1),
             whole(2, panel, rows_dev), whole(panel, panel), whole(2, panel, panel),
         ],
         out_specs=rows(step * logits, rows_dev),
         compiler_params=pltpu.CompilerParams(vmem_limit_bytes=40 * 1024 * 1024),
     )(
-        *cut(pick), *cut(top), project.reshape(images * logits, 1), gathered, corner, inverses
+        pick, pick, pick, top, top, top, project.reshape(images * logits, 1), gathered, corner, inverses
     )
 
 
@@ -480,7 +485,7 @@
     if fits:
         pick, top, project, gathered, corner = fused_front(
             normed, residual_in, w_up, w_down, final_gain[None, :], head_cols.T,
-            sub_inputs[None, :], local_hidden[None, :], panels, members,
+            sub_inputs[None, :], sub_hidden[None, :], panels, members,
         )
     else:
         gathered = lax.all_gather(panels, "dp", axis=1, tiled=True)

time: 105 us -> 105 us (level)
  other arithmetic: 1.28 us -> 0 us
    unnamed x6 -> x10, local copies, waits for them, and re-layouts: 0.01 us -> 4.15 us
    slice x4 -> x0, local copies, waits for them, and re-layouts: 3.76 us -> none  [the longest x2 2.05 us: cut(): values[images + logits:]]
    sub x1 -> x0, other arithmetic: 1.28 us -> none  [body(): local_hidden = sub_hidden - tensor_rank * hidden_dev]
where the time goes in v5:
time: 105 us; the launch traced here: 104 us
  Pallas kernels  97.6 us (93%)
  local copies, waits for them, and re-layouts  6.49 us (6%)
    pallas_call x1, Pallas kernels, fused_front(): pl.pallas_call(functools.partial(front_kernel, planes, panel), out_shape=...  93.5 us
    unnamed x10, local copies, waits for them, and re-layouts  4.15 us
    pallas_call x1, Pallas kernels, tail(): pl.pallas_call(functools.partial(tail_kernel, panel), grid=(images // ste...  4.1 us

profile of v5, /device:TPU:0, one launch (start us, length us, event | category | flops | bytes accessed | tf_op | source)
XLA Modules:
  0.0 104.1 jit_solution(8506577459727740770)
XLA Ops:
  0.0 1.3 %broadcast_in_dim.9.gain_ref = f32[1,1280]{1,0:T(1,128)} reshape(f32[1280]{0:T(1024)} %param.14) | data formatting | bytes 10240 | tf_op jit(solution)/shard_map/broadcast_in_dim | solution.py:487
  1.3 0.0 copy-start.3
  1.3 93.5 %shard_map.100 = (f32[144,1024]{1,0:T(8,128)}, f32[144,512]{1,0:T(8,128)}, f32[64,16]{1,0:T(8,128)}, bf16[2,256,1024]{2,1,0:T(8,128)(2,1)}, bf16[256,256]{1,0:T(8,128)(2,1)}) custom-call(bf16[64,1280]{1,0:T(8,128)(2,1)} %normed_hbm.1, bf16[64,1280]{1,0:T(8,128)(2,1)} %resid_hbm.1, bf16[80,2560]{1,0:T(8,128)(2,1)} %wup_ref.1, bf16[80,2560]{1,0:T(8,128)(2,1)} %bitcast.5, ...), custom_call_target="tpu_custom_call" | custom-call | flops 3355443200 | bytes 163840000 | tf_op jit(solution)/shard_map/pallas_call | solution.py:304
  94.8 1.0 %reshape.8.project_ref = f32[1024,1]{1,0:T(8,128)S(1)} reshape(f32[64,16]{1,0:T(8,128)} %get-tuple-element.12) | data formatting | bytes 8192 | tf_op jit(solution)/shard_map/reshape | solution.py:428
  95.9 0.0 copy-done.3
  95.9 0.0 copy-start
  95.9 1.1 %copy-done = f32[144,1024]{1,0:T(8,128)S(1)} copy-done((f32[144,1024]{1,0:T(8,128)S(1)}, f32[144,1024]{1,0:T(8,128)}, u32[]{:S(2)}) %copy-start) | copy-done | bytes 589848
  96.9 0.0 copy-start.1
  96.9 1.0 copy-done.1
  97.9 0.0 copy-start.2
  97.9 1.2 %copy-done.2 = bf16[2,256,1024]{2,1,0:T(8,128)(2,1)S(1)} copy-done((bf16[2,256,1024]{2,1,0:T(8,128)(2,1)S(1)}, bf16[2,256,1024]{2,1,0:T(8,128)(2,1)}, u32[]{:S(2)}) %copy-start.2) | copy-done | bytes 1048600
  99.1 0.0 copy-start.4
  99.1 0.9 copy-done.4
  100.0 4.1 %shard_map.101 = bf16[1024,1024]{1,0:T(8,128)(2,1)} custom-call(f32[144,1024]{1,0:T(8,128)S(1)} %copy-done, f32[144,1024]{1,0:T(8,128)S(1)} %copy-done, f32[144,1024]{1,0:T(8,128)S(1)} %copy-done, f32[144,512]{1,0:T(8,128)S(1)} %copy-done.1, f32[144,512]{1,0:T(8,128)S(1)} %copy-done.1, f32[144,512]{1,0:T(8,128)S(1)} %copy-done.1, ...), custom_call_target="tpu_custom_call" | custom-call | tf_op jit(solution)/shard_map/pallas_call | solution.py:415
Async XLA Ops:
  1.3 94.6 %copy-start.3 = (bf16[2,256,256]{2,1,0:T(8,128)(2,1)S(1)}, bf16[2,256,256]{2,1,0:T(8,128)(2,1)}, u32[]{:S(2)}) copy-start(bf16[2,256,256]{2,1,0:T(8,128)(2,1)} %inverses_ref.1) | copy-start | bytes 786436
  95.9 1.1 %copy-start = (f32[144,1024]{1,0:T(8,128)S(1)}, f32[144,1024]{1,0:T(8,128)}, u32[]{:S(2)}) copy-start(f32[144,1024]{1,0:T(8,128)} %get-tuple-element.10.gain_ref.bent_ref.head_ref) | copy-start | bytes 1769476
  96.9 1.0 copy-start.1
  97.9 1.2 %copy-start.2 = (bf16[2,256,1024]{2,1,0:T(8,128)(2,1)S(1)}, bf16[2,256,1024]{2,1,0:T(8,128)(2,1)}, u32[]{:S(2)}) copy-start(bf16[2,256,1024]{2,1,0:T(8,128)(2,1)} %get-tuple-element.13.panels_ref) | copy-start | bytes 3145732
  99.1 0.9 copy-start.4
